TPU v7x, 32 devices: a whole 2x2x4 slice. The times are simulated.
32 devices in a mesh: dp: 8 (over z, y), level: 4 (over x, core).
Axes of the slice: x: 2, y: 2, z: 4, core: 2. Of those that a mesh axis runs over, the one named last changes fastest.
Arguments:
- queries: bfloat16 [4800, 256], P('dp'), may hold values from -6 to 6
- memory: bfloat16 [16, 4, 16700, 256], P('dp', 'level'), may hold values from -6 to 6
- frame_size: int32 [16, 2], P('dp'), may hold values from 60 to 167, as said below
- sample_pick: int32 [4800, 4, 64], P('dp', 'level'), may hold values from 0 to 32767
- target_box: float32 [16, 32, 4], P('dp'), as said below
- match: int32 [16, 32], P('dp'), may hold values from 0 to 299, as said below
- obj_count: int32 [16], P('dp'), may hold values from 1 to 32
- w_query: float32 [256, 384], P('dp'), may hold values from -0.375 to 0.375
- w_square: float32 [12, 256, 256], P(None, 'dp')
- w_ffn_in: float32 [2, 256, 1024], P(None, 'dp'), may hold values from -0.375 to 0.375
- w_ffn_out: float32 [2, 1024, 256], P(None, 'dp'), may hold values from -0.1875 to 0.1875
- vectors: float32 [21, 256], P(None, 'dp')
- m_query: float32 [256, 384], P('dp'), may hold values from -0.1875 to 0.1875
- m_square: float32 [12, 256, 256], P(None, 'dp'), may hold values from -0.1875 to 0.1875
- m_ffn_in: float32 [2, 256, 1024], P(None, 'dp'), may hold values from -0.1875 to 0.1875
- m_ffn_out: float32 [2, 1024, 256], P(None, 'dp'), may hold values from -0.1875 to 0.1875
- m_vectors: float32 [21, 256], P(None, 'dp'), may hold values from -0.1875 to 0.1875
- a_query: float32 [256, 384], P('dp'), may hold values from -0.375 to 0.375
- a_square: float32 [12, 256, 256], P(None, 'dp'), may hold values from -0.375 to 0.375
- a_ffn_in: float32 [2, 256, 1024], P(None, 'dp'), may hold values from -0.375 to 0.375
- a_ffn_out: float32 [2, 1024, 256], P(None, 'dp'), may hold values from -0.1875 to 0.1875
- a_vectors: float32 [21, 256], P(None, 'dp'), may hold values from 0.5 to 1.5
Outputs:
- loss_sum: float32 [], replicated
- object_total: float32 [], replicated
- query_weight: float32 [256, 384], P('dp')
- query_copy: bfloat16 [256, 384], P('dp')
- query_moment: float32 [256, 384], P('dp')
- query_average: float32 [256, 384], P('dp')
- square_weight: float32 [12, 256, 256], P(None, 'dp')
- square_copy: bfloat16 [12, 256, 256], P(None, 'dp')
- square_moment: float32 [12, 256, 256], P(None, 'dp')
- square_average: float32 [12, 256, 256], P(None, 'dp')
- ffn_in_weight: float32 [2, 256, 1024], P(None, 'dp')
- ffn_in_copy: bfloat16 [2, 256, 1024], P(None, 'dp')
- ffn_in_moment: float32 [2, 256, 1024], P(None, 'dp')
- ffn_in_average: float32 [2, 256, 1024], P(None, 'dp')
- ffn_out_weight: float32 [2, 1024, 256], P(None, 'dp')
- ffn_out_copy: bfloat16 [2, 1024, 256], P(None, 'dp')
- ffn_out_moment: float32 [2, 1024, 256], P(None, 'dp')
- ffn_out_average: float32 [2, 1024, 256], P(None, 'dp')
- vector_weight: float32 [21, 256], P(None, 'dp')
- vector_copy: bfloat16 [21, 256], P(None, 'dp')
- vector_moment: float32 [21, 256], P(None, 'dp')
- vector_average: float32 [21, 256], P(None, 'dp')
Inputs may be any that keep to these rules, and one draw needn't show every extreme that they name: `frame_size`: column 0 is the rows, column 1 the columns of the finest grid; rows lie in 60 to 100, columns in 80 to 167. `match`: distinct queries within a frame. `target_box`: centres lie in 0.2 to 0.8, widths and heights in 0.05 to 0.4.
All inputs are finite; a program needn't handle non-finite values.
Results may differ from a plain program's by a relative error of at most 0.019.
Values may be sent and summed in bfloat16 or wider, within the bound.
No kernel may reach another device: no remote copies, remote signals or barrier semaphores. Data moves between devices by JAX's collectives and lax.ppermute only.
A program may use at most 384 MiB of HBM per device.

v0:
```python
import jax
import jax.numpy as jnp
from jax import lax
from jax.sharding import PartitionSpec as P

D = 256
H = 8
P_SIZE = 4
Q = 300
MCAP = 16700


HIGHEST = lax.Precision.HIGHEST
LEARNING_RATE = 2.0
MOMENTUM = 0.5
AVERAGING = 0.5
EPSILON = 1e-05
SMOOTHING = 1e-06


def plain_round(value):
    return lax.optimization_barrier(value.astype(jnp.bfloat16)).astype(jnp.float32)


def same_value(value):
    return value


def low_keep(value):
    return (plain_round(value), None)


def low_pass(kept, grad):
    return (grad,)


def back_keep(value):
    return (value, None)


def back_low(kept, grad):
    return (plain_round(grad),)


def low(value):
    rounding = jax.custom_vjp(plain_round)
    rounding.defvjp(low_keep, low_pass)
    return rounding(value)


def low_back(value):
    passing = jax.custom_vjp(same_value)
    passing.defvjp(back_keep, back_low)
    return passing(value)


def product(left, right):
    return low_back(jnp.dot(left, right, preferred_element_type=jnp.float32))


def layer_norm(values, gain, shift):
    centred = values - jnp.mean(values, -1, keepdims=True)
    spread = jnp.mean(centred * centred, -1, keepdims=True)
    return centred * lax.rsqrt(spread + EPSILON) * gain + shift


def attend(inputs, w_four, bias_out, gain, shift):
    rows = inputs.shape[0]
    shaped = low(inputs)

    def heads(weight):
        return low(product(shaped, weight)).reshape(rows // Q, Q, H, D // H)

    query_part, key_part, value_part = (heads(w_four[0]), heads(w_four[1]), heads(w_four[2]))
    scores = low_back(
        jnp.einsum("fqhe,fkhe->fhqk", query_part, key_part, preferred_element_type=jnp.float32)
    ) * (D // H) ** (-0.5)
    weights = low(jax.nn.softmax(scores, -1))
    mixed = low(
        low_back(
            jnp.einsum("fhqk,fkhe->fqhe", weights, value_part, preferred_element_type=jnp.float32)
        )
    ).reshape(rows, D)
    return layer_norm(inputs + product(mixed, w_four[3]) + bias_out, gain, shift)


def smooth_max(first, second):
    return 0.5 * (first + second + jnp.sqrt((first - second) ** 2 + SMOOTHING))


def smooth_min(first, second):
    return 0.5 * (first + second - jnp.sqrt((first - second) ** 2 + SMOOTHING))


def box_cost(picked, target):
    differ = picked - target
    distance = jnp.sum(jnp.sqrt(differ * differ + 0.01), -1)
    pred_lower = picked[:, :2] - 0.5 * picked[:, 2:]
    pred_upper = picked[:, :2] + 0.5 * picked[:, 2:]
    targ_lower = target[:, :2] - 0.5 * target[:, 2:]
    targ_upper = target[:, :2] + 0.5 * target[:, 2:]
    intersection = smooth_max(
        smooth_min(pred_upper, targ_upper) - smooth_max(pred_lower, targ_lower), 0.0
    )
    inter = intersection[:, 0] * intersection[:, 1]
    union = picked[:, 2] * picked[:, 3] + target[:, 2] * target[:, 3] - inter
    enclose = smooth_max(pred_upper, targ_upper) - smooth_min(pred_lower, targ_lower)
    hull = enclose[:, 0] * enclose[:, 1]
    general = inter / union - (hull - union) / hull
    return 5.0 * distance + 2.0 * (1.0 - general)


def post_loss(sampled, resid, w_square, w_in, w_back, vr, selector, targets, valid):
    first = layer_norm(resid + product(sampled, w_square[5]) + vr[11], vr[2], vr[3])
    hidden = low(jax.nn.gelu(product(low(first), w_in[0])))
    second = layer_norm(first + product(hidden, w_back[0]) + vr[12], vr[4], vr[5])
    third = attend(second, w_square[6:10], vr[13], vr[6], vr[7])
    hidden_two = low(jax.nn.gelu(product(low(third), w_in[1])))
    fourth = layer_norm(third + product(hidden_two, w_back[1]) + vr[14], vr[8], vr[9])
    box_one = low(jax.nn.gelu(product(low(fourth), w_square[10]) + vr[15]))
    box_two = low(jax.nn.gelu(product(box_one, w_square[11]) + vr[16]))
    boxes = jax.nn.sigmoid(product(box_two, jnp.transpose(vr[17:21])))
    picked = jnp.dot(selector, boxes, precision=HIGHEST)
    return jnp.sum(valid * box_cost(picked, targets))


def corner_data(frame_size, picked_cells, stride):
    row_count = picked_cells.shape[0]
    frame_of = jnp.arange(row_count, dtype=jnp.int32) // Q
    heights = ((frame_size[:, 0] + stride - 1) // stride)[frame_of][:, None]
    widths = ((frame_size[:, 1] + stride - 1) // stride)[frame_of][:, None]
    top_row = picked_cells[:, : H * P_SIZE] % jnp.maximum(heights - 1, 1)
    leftmost = picked_cells[:, H * P_SIZE :] % jnp.maximum(widths - 1, 1)
    bottom = jnp.minimum(top_row + 1, heights - 1)
    rightmost = jnp.minimum(leftmost + 1, widths - 1)
    return jnp.stack(
        [
            top_row * widths + leftmost,
            top_row * widths + rightmost,
            bottom * widths + leftmost,
            bottom * widths + rightmost,
        ],
        -1,
    )


def coef_of(frac_x, frac_y, weights):
    corner_weight = jnp.stack(
        [
            (1.0 - frac_y) * (1.0 - frac_x),
            (1.0 - frac_y) * frac_x,
            frac_y * (1.0 - frac_x),
            frac_y * frac_x,
        ],
        -1,
    )
    return weights[..., None] * corner_weight


def sampling_matrix(cell_row, coef_row):
    cell_row = cell_row.reshape(Q, P_SIZE, 4)
    coef_row = coef_row.reshape(Q, P_SIZE, 4)
    slots = jnp.arange(MCAP, dtype=jnp.int32)[None, :]
    total = jnp.zeros((Q, MCAP), jnp.float32)
    for point in range(P_SIZE):
        base = cell_row[:, point, 0]
        delta = slots - base[:, None]
        for corner in range(4):
            offset = (cell_row[:, point, corner] - base)[:, None]
            total = total + jnp.where(delta == offset, coef_row[:, point, corner][:, None], 0.0)
    return total


def pick_entries(cell_row, dense):
    cell_row = cell_row.reshape(Q, P_SIZE, 4)
    slots = jnp.arange(MCAP, dtype=jnp.int32)[None, :]
    picked = []
    for point in range(P_SIZE):
        base = cell_row[:, point, 0]
        delta = slots - base[:, None]
        for corner in range(4):
            offset = (cell_row[:, point, corner] - base)[:, None]
            picked.append(jnp.sum(jnp.where(delta == offset, dense, 0.0), 1))
    return jnp.stack(picked, 1)


def sample_forward(items):
    cell_row, coef_row, table = items
    return jnp.dot(
        sampling_matrix(cell_row, coef_row), table.astype(jnp.float32), precision=HIGHEST
    )


def sample_backward(items):
    cell_row, coef_row, table, grad_row = items
    table_wide = table.astype(jnp.float32)
    dense = jnp.dot(grad_row, jnp.transpose(table_wide), precision=HIGHEST)
    grad_coef = pick_entries(cell_row, dense)
    grad_table = jnp.dot(
        jnp.transpose(sampling_matrix(cell_row, coef_row)), grad_row, precision=HIGHEST
    )
    return (grad_coef, grad_table)


def update(master, gradient, moment, average):
    moment_new = MOMENTUM * moment + gradient
    master_new = master - LEARNING_RATE * (gradient + MOMENTUM * moment_new)
    average_new = AVERAGING * average + (1.0 - AVERAGING) * master_new
    return (master_new, master_new.astype(jnp.bfloat16), moment_new, average_new)


def shards(
    queries,
    memory,
    frame_size,
    sample_pick,
    target_box,
    match,
    obj_count,
    w_query,
    w_square,
    w_ffn_in,
    w_ffn_out,
    vectors,
    m_query,
    m_square,
    m_ffn_in,
    m_ffn_out,
    m_vectors,
    a_query,
    a_square,
    a_ffn_in,
    a_ffn_out,
    a_vectors,
):
    query_half, square_half, ffn_in_half, ffn_out_half, vector_half = (
        lax.all_gather(w_query.astype(jnp.bfloat16), "dp", axis=0, tiled=True),
        lax.all_gather(w_square.astype(jnp.bfloat16), "dp", axis=1, tiled=True),
        lax.all_gather(w_ffn_in.astype(jnp.bfloat16), "dp", axis=1, tiled=True),
        lax.all_gather(w_ffn_out.astype(jnp.bfloat16), "dp", axis=1, tiled=True),
        lax.all_gather(vectors.astype(jnp.bfloat16), "dp", axis=1, tiled=True),
    )
    tok_count, width = queries.shape
    frame_count, object_count = match.shape
    head_width = width // H
    level_count = lax.axis_size("level")
    level_index = lax.axis_index("level")
    per_level = H * P_SIZE
    columns = level_count * per_level
    keep_share = (level_index == 0).astype(jnp.float32)
    object_total = lax.psum(jnp.sum(obj_count).astype(jnp.float32), "dp")
    square_full = square_half.astype(jnp.float32)
    vector_full = vector_half.astype(jnp.float32)
    inputs = queries.astype(jnp.float32)

    def front(square_all, vector_rows):
        return attend(inputs, square_all[0:4], vector_rows[10], vector_rows[0], vector_rows[1])

    decoded, front_back = jax.vjp(front, square_full, vector_full)

    def project(rows_in, weight):
        return product(low(rows_in), weight)

    projected, project_back = jax.vjp(project, decoded, query_half.astype(jnp.float32))
    memory_rows = memory.reshape(frame_count * MCAP, width)
    values = jnp.dot(memory_rows, square_half[4], preferred_element_type=jnp.float32).astype(
        jnp.bfloat16
    )
    value_heads = values.reshape(frame_count, MCAP, H, head_width).transpose(0, 2, 1, 3)
    frac_x = jax.nn.sigmoid(
        lax.dynamic_slice_in_dim(projected, level_index * per_level, per_level, 1)
    )
    frac_y = jax.nn.sigmoid(
        lax.dynamic_slice_in_dim(projected, columns + level_index * per_level, per_level, 1)
    )
    logits = (
        projected[:, 2 * columns :].reshape(tok_count, level_count, H, P_SIZE).transpose(0, 2, 1, 3)
    )
    attention = jax.nn.softmax(logits.reshape(tok_count, H, level_count * P_SIZE), -1)
    own_weights = lax.dynamic_slice_in_dim(attention, level_index * P_SIZE, P_SIZE, 2).reshape(
        tok_count, per_level
    )
    stride = jnp.left_shift(jnp.int32(1), level_index)
    corners = corner_data(frame_size, sample_pick[:, 0, :], stride)

    def by_head(array):
        return array.reshape(frame_count, Q, H, P_SIZE * 4).transpose(0, 2, 1, 3)

    coefs, coef_back = jax.vjp(coef_of, frac_x, frac_y, own_weights)
    cell_heads = by_head(corners)
    coef_heads = by_head(coefs)
    level_heads = lax.map(
        lambda items: lax.map(sample_forward, items), (cell_heads, coef_heads, value_heads)
    )
    level_part = level_heads.transpose(0, 2, 1, 3).reshape(tok_count, width)
    sampled = plain_round(lax.psum(level_part.astype(jnp.bfloat16), "level").astype(jnp.float32))
    target_rows = (jnp.arange(frame_count, dtype=jnp.int32)[:, None] * Q + match).reshape(-1)
    selector = (target_rows[:, None] == jnp.arange(tok_count, dtype=jnp.int32)[None, :]).astype(
        jnp.float32
    )
    valid = (
        (jnp.arange(object_count, dtype=jnp.int32)[None, :] < obj_count[:, None])
        .astype(jnp.float32)
        .reshape(-1)
    )
    targets = target_box.reshape(-1, 4)

    def loss_of(part_sampled, resid, square_all, w_in, w_back, vector_rows):
        return post_loss(
            part_sampled, resid, square_all, w_in, w_back, vector_rows, selector, targets, valid
        )

    loss_local, post_back = jax.vjp(
        loss_of,
        sampled,
        decoded,
        square_full,
        ffn_in_half.astype(jnp.float32),
        ffn_out_half.astype(jnp.float32),
        vector_full,
    )
    grad_sampled, grad_resid, grad_sq_post, grad_in, grad_back, grad_vec_post = post_back(
        jnp.float32(1.0) / object_total
    )
    loss_sum = lax.psum(loss_local * keep_share, ("dp", "level"))
    back_half = plain_round(grad_sampled)
    grad_heads = back_half.reshape(frame_count, Q, H, head_width).transpose(0, 2, 1, 3)
    grad_coef_heads, grad_table_heads = lax.map(
        lambda items: lax.map(sample_backward, items),
        (cell_heads, coef_heads, value_heads, grad_heads),
    )
    grad_coefs = grad_coef_heads.transpose(0, 2, 1, 3).reshape(tok_count, per_level, 4)
    grad_x, grad_y, grad_weights = coef_back(grad_coefs)
    weighted = (own_weights * grad_weights).reshape(tok_count, H, P_SIZE)
    shared = lax.psum(jnp.sum(weighted, -1), "level")
    grad_logits = (
        weighted - own_weights.reshape(tok_count, H, P_SIZE) * shared[:, :, None]
    ).reshape(tok_count, per_level)
    grad_projected = jnp.zeros((tok_count, 3 * columns), jnp.float32)
    grad_projected = lax.dynamic_update_slice_in_dim(
        grad_projected, grad_x * frac_x * (1.0 - frac_x), level_index * per_level, 1
    )
    grad_projected = lax.dynamic_update_slice_in_dim(
        grad_projected, grad_y * frac_y * (1.0 - frac_y), columns + level_index * per_level, 1
    )
    grad_projected = lax.dynamic_update_slice_in_dim(
        grad_projected, grad_logits, 2 * columns + level_index * per_level, 1
    )
    grad_decoded_part, grad_query = project_back(grad_projected)
    grad_decoded = grad_resid + lax.psum(grad_decoded_part.astype(jnp.bfloat16), "level").astype(
        jnp.float32
    )
    grad_sq_front, grad_vec_front = front_back(grad_decoded)
    grad_values = (
        grad_table_heads.transpose(0, 2, 1, 3)
        .reshape(frame_count * MCAP, width)
        .astype(jnp.bfloat16)
    )
    grad_value = jnp.einsum(
        "md,me->de", memory_rows, grad_values, preferred_element_type=jnp.float32
    )
    grad_square = ((grad_sq_post + grad_sq_front) * keep_share).at[4].add(grad_value)
    grad_ffn_in = grad_in * keep_share
    grad_ffn_out = grad_back * keep_share
    grad_vectors = (grad_vec_post + grad_vec_front) * keep_share
    totals = (
        lax.psum(grad_query.astype(jnp.bfloat16), "level").astype(jnp.float32),
        lax.psum(grad_square.astype(jnp.bfloat16), "level").astype(jnp.float32),
        lax.psum(grad_ffn_in.astype(jnp.bfloat16), "level").astype(jnp.float32),
        lax.psum(grad_ffn_out.astype(jnp.bfloat16), "level").astype(jnp.float32),
        lax.psum(grad_vectors.astype(jnp.bfloat16), "level").astype(jnp.float32),
    )
    shares = (
        lax.psum_scatter(totals[0], "dp", scatter_dimension=0, tiled=True),
        lax.psum_scatter(totals[1], "dp", scatter_dimension=1, tiled=True),
        lax.psum_scatter(totals[2], "dp", scatter_dimension=1, tiled=True),
        lax.psum_scatter(totals[3], "dp", scatter_dimension=1, tiled=True),
        lax.psum_scatter(totals[4], "dp", scatter_dimension=1, tiled=True),
    )
    upd_query = update(w_query, shares[0], m_query, a_query)
    upd_square = update(w_square, shares[1], m_square, a_square)
    upd_in = update(w_ffn_in, shares[2], m_ffn_in, a_ffn_in)
    upd_out = update(w_ffn_out, shares[3], m_ffn_out, a_ffn_out)
    upd_vector = update(vectors, shares[4], m_vectors, a_vectors)
    return (
        loss_sum,
        object_total,
        upd_query[0],
        upd_query[1],
        upd_query[2],
        upd_query[3],
        upd_square[0],
        upd_square[1],
        upd_square[2],
        upd_square[3],
        upd_in[0],
        upd_in[1],
        upd_in[2],
        upd_in[3],
        upd_out[0],
        upd_out[1],
        upd_out[2],
        upd_out[3],
        upd_vector[0],
        upd_vector[1],
        upd_vector[2],
        upd_vector[3],
    )


def solution(mesh):
    return jax.shard_map(
        shards,
        mesh=mesh,
        in_specs=(
            P("dp", None),
            P("dp", "level", None, None),
            P("dp", None),
            P("dp", "level", None),
            P("dp", None, None),
            P("dp", None),
            P("dp"),
            P("dp", None),
            P(None, "dp", None),
            P(None, "dp", None),
            P(None, "dp", None),
            P(None, "dp"),
            P("dp", None),
            P(None, "dp", None),
            P(None, "dp", None),
            P(None, "dp", None),
            P(None, "dp"),
            P("dp", None),
            P(None, "dp", None),
            P(None, "dp", None),
            P(None, "dp", None),
            P(None, "dp"),
        ),
        out_specs=(
            P(),
            P(),
            P("dp", None),
            P("dp", None),
            P("dp", None),
            P("dp", None),
            P(None, "dp", None),
            P(None, "dp", None),
            P(None, "dp", None),
            P(None, "dp", None),
            P(None, "dp", None),
            P(None, "dp", None),
            P(None, "dp", None),
            P(None, "dp", None),
            P(None, "dp", None),
            P(None, "dp", None),
            P(None, "dp", None),
            P(None, "dp", None),
            P(None, "dp"),
            P(None, "dp"),
            P(None, "dp"),
            P(None, "dp"),
        ),
        check_vma=False,
    )
```

profile of v0, /device:TPU:0, one launch (start us, length us, event | category | flops | bytes accessed | tf_op | source)
XLA Modules:
  0.0 3843.7 jit_solution(15630026982679101820)
XLA Ops:
  202.2 67.5 %copy.291 = bf16[2,8,16700,32]{3,2,1,0:T(8,128)(2,1)} copy(bf16[2,8,16700,32]{2,0,3,1:T(2,128)(2,1)} %bitcast.535) | data formatting | bytes 34201600 | tf_op jit(solution)/shard_map/while | solution.py:292
  269.8 1093.3 %while.46 = (s32[]{:T(128)}, bf16[2,8,300,32]{2,3,1,0:T(8,128)(2,1)}, s32[2,8,300,16]{2,3,1,0:T(8,128)S(1)}, f32[2,8,300,16]{2,3,1,0:T(8,128)S(1)}, bf16[2,8,167...) while((s32[]{:T(128)}, bf16[2,8,300,32]{2,3,1,0:T(8,128)(2,1)}, ...), condition=%wide.region_9.11_spmd, body=%wide.region_6.10_spmd.sunk | while | flops 2179353600 | bytes 32274152 | solution.py:292
  293.8 521.8 %while.49 = (s32[]{:T(128)}, bf16[8,300,32]{1,2,0:T(8,128)(2,1)S(1)}, s32[8,300,16]{1,2,0:T(8,128)S(1)}, f32[8,300,16]{1,2,0:T(8,128)S(1)}, bf16[8,16700,32]{2,1,0:T(8,128)(2,1)}, /*index=5*/s32[]{:T(128)}) while((s32[]{:T(128)}, bf16[8,300,32]{1,2,0:T(8,128)(2,1)S(1)}, s32[8,300,16]{1,2,0:T(8,128)S(1)}, f32[8,300,16]{1,2,0:T(8,128)S(1)}, ...), condition=%wide.region_8.9_spmd, body=%wide.region_7.0_spmd.sunk | while | flops 2179353600 | bytes 6792605 | solution.py:293
  297.1 61.9 %fusion.549 = bf16[8,300,32]{1,2,0:T(8,128)(2,1)S(1)} fusion(bf16[8,300,32]{1,2,0:T(8,128)(2,1)S(1)} %get-tuple-element.969, s32[]{:T(128)S(6)} %copy.446, f32[300]{0:T(512)S(1)} %get-tuple-element.894, s32[300]{0:T(512)S(1)} %get-tuple-element.903, f32[300]{0:T(512)S(1)} %get-tuple-element.904, s32[300]{0:T(512)S(1)} %get-tuple-element.905, ...), kind=kOutput, calls=%fused_computation.89.clone.3 | convolution fusion | flops 2179350016 | bytes 4390916 | tf_op jit(solution)/shard_map/while/body/eval_jaxpr/while/body/eval_jaxpr/dot_general | solution.py:189
  362.4 61.9 %fusion.549 = bf16[8,300,32]{1,2,0:T(8,128)(2,1)S(1)} fusion(bf16[8,300,32]{1,2,0:T(8,128)(2,1)S(1)} %get-tuple-element.969, s32[]{:T(128)S(6)} %copy.446, f32[300]{0:T(512)S(1)} %get-tuple-element.894, s32[300]{0:T(512)S(1)} %get-tuple-element.903, f32[300]{0:T(512)S(1)} %get-tuple-element.904, s32[300]{0:T(512)S(1)} %get-tuple-element.905, ...), kind=kOutput, calls=%fused_computation.89.clone.3 | convolution fusion | flops 2179350016 | bytes 4390916 | tf_op jit(solution)/shard_map/while/body/eval_jaxpr/while/body/eval_jaxpr/dot_general | solution.py:189
  427.6 61.9 %fusion.549 = bf16[8,300,32]{1,2,0:T(8,128)(2,1)S(1)} fusion(bf16[8,300,32]{1,2,0:T(8,128)(2,1)S(1)} %get-tuple-element.969, s32[]{:T(128)S(6)} %copy.446, f32[300]{0:T(512)S(1)} %get-tuple-element.894, s32[300]{0:T(512)S(1)} %get-tuple-element.903, f32[300]{0:T(512)S(1)} %get-tuple-element.904, s32[300]{0:T(512)S(1)} %get-tuple-element.905, ...), kind=kOutput, calls=%fused_computation.89.clone.3 | convolution fusion | flops 2179350016 | bytes 4390916 | tf_op jit(solution)/shard_map/while/body/eval_jaxpr/while/body/eval_jaxpr/dot_general | solution.py:189
  492.8 61.9 %fusion.549 = bf16[8,300,32]{1,2,0:T(8,128)(2,1)S(1)} fusion(bf16[8,300,32]{1,2,0:T(8,128)(2,1)S(1)} %get-tuple-element.969, s32[]{:T(128)S(6)} %copy.446, f32[300]{0:T(512)S(1)} %get-tuple-element.894, s32[300]{0:T(512)S(1)} %get-tuple-element.903, f32[300]{0:T(512)S(1)} %get-tuple-element.904, s32[300]{0:T(512)S(1)} %get-tuple-element.905, ...), kind=kOutput, calls=%fused_computation.89.clone.3 | convolution fusion | flops 2179350016 | bytes 4390916 | tf_op jit(solution)/shard_map/while/body/eval_jaxpr/while/body/eval_jaxpr/dot_general | solution.py:189
  558.0 61.9 %fusion.549 = bf16[8,300,32]{1,2,0:T(8,128)(2,1)S(1)} fusion(bf16[8,300,32]{1,2,0:T(8,128)(2,1)S(1)} %get-tuple-element.969, s32[]{:T(128)S(6)} %copy.446, f32[300]{0:T(512)S(1)} %get-tuple-element.894, s32[300]{0:T(512)S(1)} %get-tuple-element.903, f32[300]{0:T(512)S(1)} %get-tuple-element.904, s32[300]{0:T(512)S(1)} %get-tuple-element.905, ...), kind=kOutput, calls=%fused_computation.89.clone.3 | convolution fusion | flops 2179350016 | bytes 4390916 | tf_op jit(solution)/shard_map/while/body/eval_jaxpr/while/body/eval_jaxpr/dot_general | solution.py:189
  623.3 61.9 %fusion.549 = bf16[8,300,32]{1,2,0:T(8,128)(2,1)S(1)} fusion(bf16[8,300,32]{1,2,0:T(8,128)(2,1)S(1)} %get-tuple-element.969, s32[]{:T(128)S(6)} %copy.446, f32[300]{0:T(512)S(1)} %get-tuple-element.894, s32[300]{0:T(512)S(1)} %get-tuple-element.903, f32[300]{0:T(512)S(1)} %get-tuple-element.904, s32[300]{0:T(512)S(1)} %get-tuple-element.905, ...), kind=kOutput, calls=%fused_computation.89.clone.3 | convolution fusion | flops 2179350016 | bytes 4390916 | tf_op jit(solution)/shard_map/while/body/eval_jaxpr/while/body/eval_jaxpr/dot_general | solution.py:189
  688.5 61.9 %fusion.549 = bf16[8,300,32]{1,2,0:T(8,128)(2,1)S(1)} fusion(bf16[8,300,32]{1,2,0:T(8,128)(2,1)S(1)} %get-tuple-element.969, s32[]{:T(128)S(6)} %copy.446, f32[300]{0:T(512)S(1)} %get-tuple-element.894, s32[300]{0:T(512)S(1)} %get-tuple-element.903, f32[300]{0:T(512)S(1)} %get-tuple-element.904, s32[300]{0:T(512)S(1)} %get-tuple-element.905, ...), kind=kOutput, calls=%fused_computation.89.clone.3 | convolution fusion | flops 2179350016 | bytes 4390916 | tf_op jit(solution)/shard_map/while/body/eval_jaxpr/while/body/eval_jaxpr/dot_general | solution.py:189
  753.7 61.9 %fusion.549 = bf16[8,300,32]{1,2,0:T(8,128)(2,1)S(1)} fusion(bf16[8,300,32]{1,2,0:T(8,128)(2,1)S(1)} %get-tuple-element.969, s32[]{:T(128)S(6)} %copy.446, f32[300]{0:T(512)S(1)} %get-tuple-element.894, s32[300]{0:T(512)S(1)} %get-tuple-element.903, f32[300]{0:T(512)S(1)} %get-tuple-element.904, s32[300]{0:T(512)S(1)} %get-tuple-element.905, ...), kind=kOutput, calls=%fused_computation.89.clone.3 | convolution fusion | flops 2179350016 | bytes 4390916 | tf_op jit(solution)/shard_map/while/body/eval_jaxpr/while/body/eval_jaxpr/dot_general | solution.py:189
  840.1 521.8 %while.49 = (s32[]{:T(128)}, bf16[8,300,32]{1,2,0:T(8,128)(2,1)S(1)}, s32[8,300,16]{1,2,0:T(8,128)S(1)}, f32[8,300,16]{1,2,0:T(8,128)S(1)}, bf16[8,16700,32]{2,1,0:T(8,128)(2,1)}, /*index=5*/s32[]{:T(128)}) while((s32[]{:T(128)}, bf16[8,300,32]{1,2,0:T(8,128)(2,1)S(1)}, s32[8,300,16]{1,2,0:T(8,128)S(1)}, f32[8,300,16]{1,2,0:T(8,128)S(1)}, ...), condition=%wide.region_8.9_spmd, body=%wide.region_7.0_spmd.sunk | while | flops 2179353600 | bytes 6792605 | solution.py:293
  843.5 61.9 %fusion.549 = bf16[8,300,32]{1,2,0:T(8,128)(2,1)S(1)} fusion(bf16[8,300,32]{1,2,0:T(8,128)(2,1)S(1)} %get-tuple-element.969, s32[]{:T(128)S(6)} %copy.446, f32[300]{0:T(512)S(1)} %get-tuple-element.894, s32[300]{0:T(512)S(1)} %get-tuple-element.903, f32[300]{0:T(512)S(1)} %get-tuple-element.904, s32[300]{0:T(512)S(1)} %get-tuple-element.905, ...), kind=kOutput, calls=%fused_computation.89.clone.3 | convolution fusion | flops 2179350016 | bytes 4390916 | tf_op jit(solution)/shard_map/while/body/eval_jaxpr/while/body/eval_jaxpr/dot_general | solution.py:189
  908.7 61.9 %fusion.549 = bf16[8,300,32]{1,2,0:T(8,128)(2,1)S(1)} fusion(bf16[8,300,32]{1,2,0:T(8,128)(2,1)S(1)} %get-tuple-element.969, s32[]{:T(128)S(6)} %copy.446, f32[300]{0:T(512)S(1)} %get-tuple-element.894, s32[300]{0:T(512)S(1)} %get-tuple-element.903, f32[300]{0:T(512)S(1)} %get-tuple-element.904, s32[300]{0:T(512)S(1)} %get-tuple-element.905, ...), kind=kOutput, calls=%fused_computation.89.clone.3 | convolution fusion | flops 2179350016 | bytes 4390916 | tf_op jit(solution)/shard_map/while/body/eval_jaxpr/while/body/eval_jaxpr/dot_general | solution.py:189
  973.9 61.9 %fusion.549 = bf16[8,300,32]{1,2,0:T(8,128)(2,1)S(1)} fusion(bf16[8,300,32]{1,2,0:T(8,128)(2,1)S(1)} %get-tuple-element.969, s32[]{:T(128)S(6)} %copy.446, f32[300]{0:T(512)S(1)} %get-tuple-element.894, s32[300]{0:T(512)S(1)} %get-tuple-element.903, f32[300]{0:T(512)S(1)} %get-tuple-element.904, s32[300]{0:T(512)S(1)} %get-tuple-element.905, ...), kind=kOutput, calls=%fused_computation.89.clone.3 | convolution fusion | flops 2179350016 | bytes 4390916 | tf_op jit(solution)/shard_map/while/body/eval_jaxpr/while/body/eval_jaxpr/dot_general | solution.py:189
  1039.1 61.9 %fusion.549 = bf16[8,300,32]{1,2,0:T(8,128)(2,1)S(1)} fusion(bf16[8,300,32]{1,2,0:T(8,128)(2,1)S(1)} %get-tuple-element.969, s32[]{:T(128)S(6)} %copy.446, f32[300]{0:T(512)S(1)} %get-tuple-element.894, s32[300]{0:T(512)S(1)} %get-tuple-element.903, f32[300]{0:T(512)S(1)} %get-tuple-element.904, s32[300]{0:T(512)S(1)} %get-tuple-element.905, ...), kind=kOutput, calls=%fused_computation.89.clone.3 | convolution fusion | flops 2179350016 | bytes 4390916 | tf_op jit(solution)/shard_map/while/body/eval_jaxpr/while/body/eval_jaxpr/dot_general | solution.py:189
  1104.3 61.9 %fusion.549 = bf16[8,300,32]{1,2,0:T(8,128)(2,1)S(1)} fusion(bf16[8,300,32]{1,2,0:T(8,128)(2,1)S(1)} %get-tuple-element.969, s32[]{:T(128)S(6)} %copy.446, f32[300]{0:T(512)S(1)} %get-tuple-element.894, s32[300]{0:T(512)S(1)} %get-tuple-element.903, f32[300]{0:T(512)S(1)} %get-tuple-element.904, s32[300]{0:T(512)S(1)} %get-tuple-element.905, ...), kind=kOutput, calls=%fused_computation.89.clone.3 | convolution fusion | flops 2179350016 | bytes 4390916 | tf_op jit(solution)/shard_map/while/body/eval_jaxpr/while/body/eval_jaxpr/dot_general | solution.py:189
  1169.6 61.9 %fusion.549 = bf16[8,300,32]{1,2,0:T(8,128)(2,1)S(1)} fusion(bf16[8,300,32]{1,2,0:T(8,128)(2,1)S(1)} %get-tuple-element.969, s32[]{:T(128)S(6)} %copy.446, f32[300]{0:T(512)S(1)} %get-tuple-element.894, s32[300]{0:T(512)S(1)} %get-tuple-element.903, f32[300]{0:T(512)S(1)} %get-tuple-element.904, s32[300]{0:T(512)S(1)} %get-tuple-element.905, ...), kind=kOutput, calls=%fused_computation.89.clone.3 | convolution fusion | flops 2179350016 | bytes 4390916 | tf_op jit(solution)/shard_map/while/body/eval_jaxpr/while/body/eval_jaxpr/dot_general | solution.py:189
  1234.8 61.9 %fusion.549 = bf16[8,300,32]{1,2,0:T(8,128)(2,1)S(1)} fusion(bf16[8,300,32]{1,2,0:T(8,128)(2,1)S(1)} %get-tuple-element.969, s32[]{:T(128)S(6)} %copy.446, f32[300]{0:T(512)S(1)} %get-tuple-element.894, s32[300]{0:T(512)S(1)} %get-tuple-element.903, f32[300]{0:T(512)S(1)} %get-tuple-element.904, s32[300]{0:T(512)S(1)} %get-tuple-element.905, ...), kind=kOutput, calls=%fused_computation.89.clone.3 | convolution fusion | flops 2179350016 | bytes 4390916 | tf_op jit(solution)/shard_map/while/body/eval_jaxpr/while/body/eval_jaxpr/dot_general | solution.py:189
  1300.0 61.9 %fusion.549 = bf16[8,300,32]{1,2,0:T(8,128)(2,1)S(1)} fusion(bf16[8,300,32]{1,2,0:T(8,128)(2,1)S(1)} %get-tuple-element.969, s32[]{:T(128)S(6)} %copy.446, f32[300]{0:T(512)S(1)} %get-tuple-element.894, s32[300]{0:T(512)S(1)} %get-tuple-element.903, f32[300]{0:T(512)S(1)} %get-tuple-element.904, s32[300]{0:T(512)S(1)} %get-tuple-element.905, ...), kind=kOutput, calls=%fused_computation.89.clone.3 | convolution fusion | flops 2179350016 | bytes 4390916 | tf_op jit(solution)/shard_map/while/body/eval_jaxpr/while/body/eval_jaxpr/dot_general | solution.py:189
  1576.6 1702.7 %while.48 = (s32[]{:T(128)}, f32[2,8,300,16]{2,3,1,0:T(8,128)}, bf16[2,8,16700,32]{2,3,1,0:T(8,128)(2,1)}, s32[2,8,300,16]{2,3,1,0:T(8,128)S(1)}, f32[2,8,300,16...) while((s32[]{:T(128)}, f32[2,8,300,16]{2,3,1,0:T(8,128)}, ...), condition=%wide.region_54.56_spmd, body=%wide.region_35.55_spmd.sunk | while | flops 4363708416 | bytes 54778448 | solution.py:328
  1620.7 808.2 %while.50 = (s32[]{:T(128)}, f32[8,300,16]{1,2,0:T(8,128)S(1)}, bf16[8,16700,32]{1,2,0:T(8,128)(2,1)}, s32[8,300,16]{1,2,0:T(8,128)S(1)}, f32[8,300,32]{2,1,0:T(...) while((s32[]{:T(128)}, f32[8,300,16]{1,2,0:T(8,128)S(1)}, ...), condition=%wide.region_53.54_spmd, body=%wide.region_36.53_spmd.sunk | while | flops 4363708416 | bytes 8483037 | solution.py:329
  1871.9 52.0 %fusion.543 = bf16[8,16700,32]{1,2,0:T(8,128)(2,1)} fusion(bf16[8,16700,32]{1,2,0:T(8,128)(2,1)} %get-tuple-element.948, s32[]{:T(128)S(6)} %copy.435, f32[300]{0:T(512)S(1)} %get-tuple-element.873, f32[300]{0:T(512)S(1)} %get-tuple-element.874, f32[300]{0:T(512)S(1)} %get-tuple-element.875, f32[300]{0:T(512)S(1)} %get-tuple-element.876, ...), kind=kOutput, calls=%fused_computation.199.clone.1 | convolution fusion | flops 2179350016 | bytes 2368512 | tf_op jit(solution)/shard_map/while/body/eval_jaxpr/while/body/eval_jaxpr/dot_general | solution.py:199
  2174.9 52.0 %fusion.543 = bf16[8,16700,32]{1,2,0:T(8,128)(2,1)} fusion(bf16[8,16700,32]{1,2,0:T(8,128)(2,1)} %get-tuple-element.948, s32[]{:T(128)S(6)} %copy.435, f32[300]{0:T(512)S(1)} %get-tuple-element.873, f32[300]{0:T(512)S(1)} %get-tuple-element.874, f32[300]{0:T(512)S(1)} %get-tuple-element.875, f32[300]{0:T(512)S(1)} %get-tuple-element.876, ...), kind=kOutput, calls=%fused_computation.199.clone.1 | convolution fusion | flops 2179350016 | bytes 2368512 | tf_op jit(solution)/shard_map/while/body/eval_jaxpr/while/body/eval_jaxpr/dot_general | solution.py:199
  2462.6 808.1 %while.50 = (s32[]{:T(128)}, f32[8,300,16]{1,2,0:T(8,128)S(1)}, bf16[8,16700,32]{1,2,0:T(8,128)(2,1)}, s32[8,300,16]{1,2,0:T(8,128)S(1)}, f32[8,300,32]{2,1,0:T(...) while((s32[]{:T(128)}, f32[8,300,16]{1,2,0:T(8,128)S(1)}, ...), condition=%wide.region_53.54_spmd, body=%wide.region_36.53_spmd.sunk | while | flops 4363708416 | bytes 8483037 | solution.py:329
  2713.7 52.0 %fusion.543 = bf16[8,16700,32]{1,2,0:T(8,128)(2,1)} fusion(bf16[8,16700,32]{1,2,0:T(8,128)(2,1)} %get-tuple-element.948, s32[]{:T(128)S(6)} %copy.435, f32[300]{0:T(512)S(1)} %get-tuple-element.873, f32[300]{0:T(512)S(1)} %get-tuple-element.874, f32[300]{0:T(512)S(1)} %get-tuple-element.875, f32[300]{0:T(512)S(1)} %get-tuple-element.876, ...), kind=kOutput, calls=%fused_computation.199.clone.1 | convolution fusion | flops 2179350016 | bytes 2368512 | tf_op jit(solution)/shard_map/while/body/eval_jaxpr/while/body/eval_jaxpr/dot_general | solution.py:199
  3016.7 52.0 %fusion.543 = bf16[8,16700,32]{1,2,0:T(8,128)(2,1)} fusion(bf16[8,16700,32]{1,2,0:T(8,128)(2,1)} %get-tuple-element.948, s32[]{:T(128)S(6)} %copy.435, f32[300]{0:T(512)S(1)} %get-tuple-element.873, f32[300]{0:T(512)S(1)} %get-tuple-element.874, f32[300]{0:T(512)S(1)} %get-tuple-element.875, f32[300]{0:T(512)S(1)} %get-tuple-element.876, ...), kind=kOutput, calls=%fused_computation.199.clone.1 | convolution fusion | flops 2179350016 | bytes 2368512 | tf_op jit(solution)/shard_map/while/body/eval_jaxpr/while/body/eval_jaxpr/dot_general | solution.py:199
  3417.3 67.4 %all-reduce.54.cloned.1.call-done = (bf16[256,384]{1,0:T(8,128)(2,1)}, bf16[12,256,256]{2,1,0:T(8,128)(2,1)}, bf16[2,256,1024]{2,1,0:T(8,128)(2,1)}, bf16[2,1024,256]{2,1,0:T(8,128)(2,1)}) async-done(((bf16[256,384]{1,0:T(8,128)(2,1)}, bf16[12,256,256]{2,1,0:T(8,128)(2,1)}, bf16[2,256,1024]{2,1,0:T(8,128)(2,1)}, bf16[2,1024,256]{2,1,0:T(8,128)(2,1)}), (bf16[256,384]{1,0:T(8,128)(2,1)}, ...) | async-done | bytes 3866640 | tf_op jit(solution)/shard_map/psum | solution.py:367
  3552.7 61.9 %reduce-scatter.8.cloned.1.call-done = f32[32,384]{1,0:T(8,128)} async-done(((f32[256,384]{1,0:T(8,128)}), f32[32,384]{1,0:T(8,128)}) %reduce-scatter.8.cloned.1.call-update) | async-done | bytes 49168 | tf_op jit(solution)/shard_map/reduce_scatter | solution.py:374
  3616.7 68.6 %reduce-scatter.12.cloned.1.call-done = f32[2,32,1024]{2,1,0:T(8,128)} async-done(((f32[2,256,1024]{2,1,0:T(8,128)}), f32[2,32,1024]{2,1,0:T(8,128)}) %reduce-scatter.12.cloned.1.call-update) | async-done | bytes 262160 | tf_op jit(solution)/shard_map/reduce_scatter | solution.py:376
  3687.9 68.0 %reduce-scatter.14.cloned.1.call-done = f32[2,128,256]{2,1,0:T(8,128)} async-done(((f32[2,1024,256]{2,1,0:T(8,128)}), f32[2,128,256]{2,1,0:T(8,128)}) %reduce-scatter.14.cloned.1.call-update) | async-done | bytes 262160 | tf_op jit(solution)/shard_map/reduce_scatter | solution.py:377
  3758.6 75.5 %reduce-scatter.10.cloned.1.call-done = f32[12,32,256]{2,1,0:T(8,128)} async-done(((f32[12,256,256]{2,1,0:T(8,128)}), f32[12,32,256]{2,1,0:T(8,128)}) %reduce-scatter.10.cloned.1.call-update) | async-done | bytes 393232 | tf_op jit(solution)/shard_map/reduce_scatter | solution.py:375
  (1301 shorter events, 2193.5 us)
Async XLA Ops:
  7.2 107.9 %all-gather.5.cloned.1.call-start = ((), (), s32[]{:S(2)}) async-start(), calls=%async_computation.5 | async-start | bytes 1769472 | tf_op jit(solution)/shard_map/all_gather | solution.py:238
  9.0 1390.0 %all-reduce.50.cloned.1.call-start = ((), (), s32[]{:S(2)}) async-start(), calls=%async_computation.6 | async-start | bytes 655360 | tf_op jit(solution)/shard_map/psum | solution.py:296
  269.7 1096.0 %copy-start.55 = (f32[2,32,1024]{2,1,0:T(8,128)S(1)}, f32[2,32,1024]{2,1,0:T(8,128)}, u32[]{:S(2)}) copy-start(f32[2,32,1024]{2,1,0:T(8,128)} %param.43) | copy-start | bytes 786436
  269.7 1096.7 %copy-start.57 = (f32[2,128,256]{2,1,0:T(8,128)S(1)}, f32[2,128,256]{2,1,0:T(8,128)}, u32[]{:S(2)}) copy-start(f32[2,128,256]{2,1,0:T(8,128)} %param.44) | copy-start | bytes 786436
  269.7 1097.5 %copy-start.137 = (s32[2]{0:T(128)S(1)}, s32[2]{0:T(128)}, u32[]{:S(2)}) copy-start(s32[2]{0:T(128)} %param.40) | copy-start | bytes 28
  269.7 1120.7 %copy-start.136 = (s32[2,32]{1,0:T(2,128)S(1)}, s32[2,32]{1,0:T(2,128)}, u32[]{:S(2)}) copy-start(s32[2,32]{1,0:T(2,128)} %param.39) | copy-start | bytes 772
  269.7 1121.7 %copy-start.118 = (f32[2,32,4]{1,2,0:T(4,128)S(1)}, f32[2,32,4]{1,2,0:T(4,128)}, u32[]{:S(2)}) copy-start(f32[2,32,4]{1,2,0:T(4,128)} %param.38) | copy-start | bytes 3076
  269.7 1121.8 %copy-start.83 = (f32[2,8,300]{2,1,0:T(8,128)S(1)}, f32[2,8,300]{2,1,0:T(8,128)}, u32[]{:S(2)}) copy-start(f32[2,8,300]{2,1,0:T(8,128)} %copy-done.82) | copy-start | bytes 57604
  269.7 1129.3 %copy-start.3 = (f32[600,256]{1,0:T(8,128)S(1)}, f32[600,256]{1,0:T(8,128)}, u32[]{:S(2)}) copy-start(f32[600,256]{1,0:T(8,128)} %copy-done.2) | copy-start | bytes 1843204
  269.7 1129.3 %copy-start.87 = (f32[600]{0:T(1024)S(1)}, f32[600]{0:T(1024)}, u32[]{:S(2)}) copy-start(f32[600]{0:T(1024)} %copy-done.86) | copy-start | bytes 7204
  269.7 1129.3 %copy-start.93 = (f32[600]{0:T(1024)S(1)}, f32[600]{0:T(1024)}, u32[]{:S(2)}) copy-start(f32[600]{0:T(1024)} %copy-done.92) | copy-start | bytes 7204
  269.7 1129.2 %copy-start.102 = (f32[1,256]{1,0:T(1,128)S(1)}, f32[1,256]{1,0:T(1,128)}, u32[]{:S(2)}) copy-start(f32[1,256]{1,0:T(1,128)} %copy-done.101) | copy-start | bytes 3076
  269.8 1129.2 %copy-start.117 = (f32[1,256]{1,0:T(1,128)S(1)}, f32[1,256]{1,0:T(1,128)}, u32[]{:S(2)}) copy-start(f32[1,256]{1,0:T(1,128)} %copy-done.116) | copy-start | bytes 3076
  269.8 1129.2 %copy-start.135 = (f32[1,256]{1,0:T(1,128)S(1)}, f32[1,256]{1,0:T(1,128)}, u32[]{:S(2)}) copy-start(f32[1,256]{1,0:T(1,128)} %get-tuple-element.492) | copy-start | bytes 3076
  269.8 1131.0 %copy-start.105 = (f32[1,256]{1,0:T(1,128)S(1)}, f32[1,256]{1,0:T(1,128)}, u32[]{:S(2)}) copy-start(f32[1,256]{1,0:T(1,128)} %get-tuple-element.491) | copy-start | bytes 3076
  269.8 1131.0 %copy-start.115 = (f32[1,256]{1,0:T(1,128)S(1)}, f32[1,256]{1,0:T(1,128)}, u32[]{:S(2)}) copy-start(f32[1,256]{1,0:T(1,128)} %get-tuple-element.490) | copy-start | bytes 3076
  293.8 522.6 %copy-start.8 = (s32[2,8,300,16]{2,3,1,0:T(8,128)S(1)}, s32[2,8,300,16]{2,3,1,0:T(8,128)}, u32[]{:S(2)}) copy-start(s32[2,8,300,16]{2,3,1,0:T(8,128)} %copy-done.7) | copy-start | bytes 921604 | tf_op jit(solution)/shard_map/while
  293.8 522.6 %copy-start.12 = (f32[2,8,300,16]{2,3,1,0:T(8,128)S(1)}, f32[2,8,300,16]{2,3,1,0:T(8,128)}, u32[]{:S(2)}) copy-start(f32[2,8,300,16]{2,3,1,0:T(8,128)} %copy-done.11) | copy-start | bytes 921604 | tf_op jit(solution)/shard_map/while
  840.1 522.6 %copy-start.8 = (s32[2,8,300,16]{2,3,1,0:T(8,128)S(1)}, s32[2,8,300,16]{2,3,1,0:T(8,128)}, u32[]{:S(2)}) copy-start(s32[2,8,300,16]{2,3,1,0:T(8,128)} %copy-done.7) | copy-start | bytes 921604 | tf_op jit(solution)/shard_map/while
  840.1 522.6 %copy-start.12 = (f32[2,8,300,16]{2,3,1,0:T(8,128)S(1)}, f32[2,8,300,16]{2,3,1,0:T(8,128)}, u32[]{:S(2)}) copy-start(f32[2,8,300,16]{2,3,1,0:T(8,128)} %copy-done.11) | copy-start | bytes 921604 | tf_op jit(solution)/shard_map/while
  1365.6 76.4 %all-gather.7.cloned.1.call-start = ((), (), s32[]{:S(2)}) async-start(), calls=%async_computation.7 | async-start | bytes 1179648 | tf_op jit(solution)/shard_map/all_gather | solution.py:239
  1366.3 117.2 %all-gather.9.cloned.1.call-start = ((), (), s32[]{:S(2)}) async-start(), calls=%async_computation.8 | async-start | bytes 1179648 | tf_op jit(solution)/shard_map/all_gather | solution.py:240
  1367.1 2000.6 %all-reduce.52.cloned.1.call-start = ((), (), s32[]{:S(2)}) async-start(), calls=%async_computation.10 | async-start | bytes 614400 | tf_op jit(solution)/shard_map/psum | solution.py:350
  1576.6 1707.9 %copy-start.73 = (f32[600,8]{0,1:T(8,128)S(1)}, f32[600,8]{0,1:T(8,128)}, u32[]{:S(2)}) copy-start(f32[600,8]{0,1:T(8,128)} %copy-done.72) | copy-start | bytes 57604
  1576.6 1720.1 %copy-start.31 = (bf16[600,256]{1,0:T(8,128)(2,1)S(1)}, bf16[600,256]{1,0:T(8,128)(2,1)}, u32[]{:S(2)}) copy-start(bf16[600,256]{1,0:T(8,128)(2,1)} %copy-done.30) | copy-start | bytes 921604
  1576.6 1721.1 %copy-start.33 = (bf16[256,384]{1,0:T(8,128)(2,1)S(1)}, bf16[256,384]{1,0:T(8,128)(2,1)}, u32[]{:S(2)}) copy-start(bf16[256,384]{1,0:T(8,128)(2,1)} %copy-done.32) | copy-start | bytes 589828
  3298.8 185.9 %all-reduce.54.cloned.1.call-start = ((), (), s32[]{:S(2)}) async-start(), calls=%async_computation.15 | async-start | bytes 7733248 | tf_op jit(solution)/shard_map/psum | solution.py:367
  3404.9 145.0 %reduce-scatter.16.cloned.1.call-start = ((), (), s32[]{:S(2)}) async-start(), calls=%async_computation.14 | async-start | bytes 147456
  3417.3 197.3 %reduce-scatter.8.cloned.1.call-start = ((), (), s32[]{:S(2)}) async-start(), calls=%async_computation.9 | async-start | bytes 442368 | tf_op jit(solution)/shard_map/reduce_scatter | solution.py:374
  3486.6 198.7 %reduce-scatter.12.cloned.1.call-start = ((), (), s32[]{:S(2)}) async-start(), calls=%async_computation.12 | async-start | bytes 2359296 | tf_op jit(solution)/shard_map/reduce_scatter | solution.py:376
  3489.5 266.5 %reduce-scatter.14.cloned.1.call-start = ((), (), s32[]{:S(2)}) async-start(), calls=%async_computation.13 | async-start | bytes 2359296 | tf_op jit(solution)/shard_map/reduce_scatter | solution.py:377
  3492.4 341.8 %reduce-scatter.10.cloned.1.call-start = ((), (), s32[]{:S(2)}) async-start(), calls=%async_computation.11 | async-start | bytes 3538944 | tf_op jit(solution)/shard_map/reduce_scatter | solution.py:375
  (169 other events, 6637.1 us)
Sparse Core Ops, SparseCore 0:
  10.8 46.8 all-gather.4
  1365.7 33.2 all-reduce.49
  1401.8 40.1 all-gather.6
  1444.6 38.9 all-gather.8
  3299.0 30.3 all-reduce.51
  3405.0 79.6 all-reduce.53
  3489.0 60.9 reduce-scatter.15
  3554.1 60.3 reduce-scatter.7
  3618.5 66.7 reduce-scatter.11
  3689.1 66.8 reduce-scatter.13
  3760.0 74.0 reduce-scatter.9
where the time goes:
time: 3860 us; the launch traced here: 3840 us
  matrix products  2720 us (70%)
  waiting for transfers between devices  441 us (11%)
  local copies, waits for them, and re-layouts  423 us (11%)
  blocking collectives  146 us (4%)
  other arithmetic  71.2 us (2%)
    dot_general x16, matrix products, sample_forward(): jnp.dot(sampling_matrix(cell_row, coef_row), table.astype(jnp.float32), p...  990 us
    dot_general x16, matrix products, sample_backward(): jnp.dot(jnp.transpose(sampling_matrix(cell_row, coef_row)), grad_row, pre...  831 us
    dot_general x16, matrix products, sample_backward(): dense = jnp.dot(grad_row, jnp.transpose(table_wide), precision=HIGHEST)  776 us
    squeeze x12, local copies, waits for them, and re-layouts, shards(): lax.map(lambda items: lax.map(sample_forward, items), (cell_heads, coef_h...  94.5 us
  transfers between devices with their start and end apart: 11, of which 9 were waited for; matrix products, arithmetic and copies ran while one was open for 4% of the time, Pallas kernels for 0%

commit v1 on v0

v1 whole, which is shorter than its diff:
```python
import jax
import jax.numpy as jnp
from jax import lax
from jax.experimental import pallas as pl
from jax.experimental.pallas import tpu as pltpu
from jax.sharding import PartitionSpec as P

D = 256
H = 8
P_SIZE = 4
Q = 300
MCAP = 16700
FR = 304
R = 2 * FR
NB = R // 4
PAD = 8
STRIDE = 168
ROWS = 100
TABLE = PAD + (ROWS + 1) * STRIDE + PAD
STAGE = 19
COPIES = 4
SHARDS = 8
RS = D // SHARDS
EARLY_BITS = (4, 2, 1)
LATE_BITS = (1, 2, 4)
BF = jnp.bfloat16
F32 = jnp.float32
VMEM_LIMIT = 62 * 1024 * 1024


def lane_iota(rows):
    return lax.broadcasted_iota(jnp.int32, (rows, 128), 1)


def dot(a, b):
    return jnp.dot(a, b, preferred_element_type=F32)


def dot_nt(a, b):
    return lax.dot_general(a, b, (((1,), (1,)), ((), ())), preferred_element_type=F32)


def dot_tn(a, b):
    return lax.dot_general(a, b, (((0,), (0,)), ((), ())), preferred_element_type=F32)


def expand_matrix(point, dy):
    row = lax.broadcasted_iota(jnp.int32, (128, 256), 0)
    col = lax.broadcasted_iota(jnp.int32, (128, 256), 1) // 32
    return (row == dy * 32 + col * 4 + point).astype(F32).astype(BF)


def fold_matrix(point):
    row = lax.broadcasted_iota(jnp.int32, (256, 128), 0) // 32
    col = lax.broadcasted_iota(jnp.int32, (256, 128), 1)
    return (col == row * 4 + point).astype(F32).astype(BF)


def join_frames(own, mine_ref, other_ref, scr):
    scr[own] = mine_ref[...]
    scr[1 - own] = other_ref[...]
    return scr[...].reshape(R, scr.shape[-1])


def place_coefs(fa, scr):
    lane = lane_iota(R)
    low = lane < 32
    r32, r64, r96 = pltpu.roll(fa, 32, 1), pltpu.roll(fa, 64, 1), pltpu.roll(fa, 96, 1)
    fx = jnp.where(low, fa, r32)
    cy = jnp.where(low, 1.0 - r96, fa)
    att = jnp.where(low, r64, r96)
    base = jnp.where(lane < 64, att * cy, 0.0)
    for dx in range(2):
        coef = base * (fx if dx else 1.0 - fx)
        for k in range(4):
            scr[pl.ds(2 * k + dx, NB, 8), :] = coef[k * NB : (k + 1) * NB]


def fill_weights(scr, wexp):
    packed = scr[...].astype(BF)
    for point in range(4):
        for dy in range(2):
            wexp[point * 2 + dy] = dot(packed, expand_matrix(point, dy)).astype(wexp.dtype)


def row_masks():
    lane = lane_iota(8) // 32
    sub = lax.broadcasted_iota(jnp.int32, (8, 128), 0)
    heads = [lane == h for h in range(4)]
    rows = [sub // 2 == k for k in range(4)]
    return heads, rows


def pick_copies(idx_ref, picks, sem):
    return [pltpu.make_async_copy(idx_ref.at[c % 4, c // 4], picks[c], sem) for c in range(128)]


class Chunks:
    def __init__(self, mem_ref, buf, stage, sems, size_ref, ids_ref):
        self.mem_ref, self.buf, self.stage, self.sems = mem_ref, buf, stage, sems
        self.cells = buf.shape[1]
        level = ids_ref[0]
        self.high, self.wide = (
            [(size_ref[f, axis] + (1 << level) - 1) >> level for f in range(2)] for axis in range(2)
        )
        used = jnp.maximum(self.high[0] * self.wide[0], self.high[1] * self.wide[1])
        self.count = lax.div(used + self.cells - 1, self.cells)
        self.inner = slice(2 * STRIDE, 2 * STRIDE + 2 * self.cells)
        self.whole = -(-MCAP // self.cells)
        self.again = self.whole * self.cells - MCAP

    def base(self, j):
        return jnp.minimum(j * self.cells, MCAP - self.cells)

    def grid_rows(self, cell, f):
        return lax.div(jnp.minimum(cell, MCAP), self.wide[f])

    def copies(self, j, slot):
        size = self.cells // COPIES
        return [
            pltpu.make_async_copy(
                self.mem_ref.at[0, pl.ds(self.base(j) + c * size, size)],
                self.buf.at[slot, pl.ds(c * size, size)],
                self.sems.at[slot, c],
            )
            for c in range(COPIES)
        ]

    def start(self, j, slot):
        for copy in self.copies(j, slot):
            copy.start()

    def staged(self, i, f, j):
        return pl.ds(2 * (i * self.wide[f] - self.base(j) + STRIDE) + f, STRIDE, 2)

    def run(self, work):
        def body(j, carry):
            slot = j % 2

            @pl.when(j + 1 < self.count)
            def _():
                self.start(j + 1, 1 - slot)

            for copy in self.copies(j, slot):
                copy.wait()
            work(j, self.buf[slot].reshape(2 * self.cells, D))
            return carry

        lax.fori_loop(0, self.count, body, 0)


def grid_row(i):
    return pl.ds(pl.multiple_of(i * STRIDE, 8) + PAD, STRIDE)


def pick_kernel(size_ref, ids_ref, pick_ref, out_ref):
    level = ids_ref[0]
    frame = lax.broadcasted_iota(jnp.int32, (1, 2 * Q), 1) >= Q

    def of_frame(column):
        first, second = ((size_ref[f, column] + (1 << level) - 1) >> level for f in range(2))
        return jnp.where(frame, second, first).astype(F32)

    def rest(values, most):
        m = jnp.maximum(most - 1.0, 1.0)
        left = values - jnp.floor(values * (1.0 / m)) * m
        left = jnp.where(left < 0.0, left + m, left)
        return jnp.where(left >= m, left - m, left)

    picks = pick_ref[...].astype(F32)
    cell = rest(picks[:32], of_frame(0)) * STRIDE + rest(picks[32:], of_frame(1))
    row = cell.astype(jnp.int32)
    for k in range(4):
        first = (k // 2) * Q + (k % 2) * NB
        width = NB if k % 2 == 0 else Q - NB
        out_ref[k, :, :width] = row[:, first : first + width]
        if width < NB:
            out_ref[k, :, width:] = jnp.zeros((32, NB - width), jnp.int32)


def pick_rows(size, ids, picks):
    return pl.pallas_call(
        pick_kernel,
        in_specs=[SM, SM, VM],
        out_specs=VM,
        out_shape=jax.ShapeDtypeStruct((4, 32, NB), jnp.int32),
        name="pick_rows",
    )(size, ids, picks)


def forward_kernel(
    idx_ref, size_ref, ids_ref, mem_ref, s4_ref, mine_ref, other_ref,
    g_ref, out_ref, send_ref,
    buf, stage, tables, wexp, racc, cscr, fscr, gscr, gtmp, sems, isem, gsems, *picks,
):
    own = ids_ref[1]
    chunks = Chunks(mem_ref, buf, stage, sems, size_ref, ids_ref)
    chunks.start(0, 0)
    for copy in pick_copies(idx_ref, picks, isem):
        copy.start()
    place_coefs(join_frames(own, mine_ref, other_ref, fscr), cscr)
    fill_weights(cscr, wexp)

    def fill(j, m):
        v = dot(m, s4_ref[...])
        for half in range(2):
            stage[half, chunks.inner, :] = v[:, half * 128 : half * 128 + 128]
        for f in range(2):
            first = chunks.grid_rows(j * chunks.cells, f)
            last = jnp.minimum(chunks.grid_rows((j + 1) * chunks.cells, f), chunks.high[f])

            def copy_row(i, carry):
                for half in range(2):
                    tables[f][half][grid_row(i), :] = stage[half, chunks.staged(i, f, j), :]
                return carry

            lax.fori_loop(first, last, copy_row, 0)
        for half in range(2):
            kept = pl.ds(2 * (chunks.base(j + 1) - chunks.base(j)), 2 * STRIDE)
            stage[half, : 2 * STRIDE, :] = stage[half, kept, :]

    chunks.run(fill)
    for copy in pick_copies(idx_ref, picks, isem):
        copy.wait()
    heads, rows = row_masks()

    def block(j):
        found = [None] * 16
        for half in range(2):
            for point in range(4):
                acc = None
                for h in range(4):
                    part = None
                    for k in range(4):
                        r = picks[((half * 4 + h) * 4 + point) * 4 + k][j] + (PAD - 2 * k)
                        table = tables[k // 2][half]
                        new = (table[pl.ds(r, 8), :], table[pl.ds(r + STRIDE, 8), :])
                        part = new if part is None else [jnp.where(rows[k], x, y) for x, y in zip(new, part)]
                    acc = part if acc is None else [jnp.where(heads[h], x, y) for x, y in zip(part, acc)]
                found[half * 8 + point * 2], found[half * 8 + point * 2 + 1] = acc
        return found

    def gather_block(j, carry):
        low = pl.ds(pl.multiple_of((j % 2) * 8, 8), 8)
        for n, found in enumerate(block(j)):
            gtmp[n, low, :] = found
        return carry

    def gather(i, carry):
        lax.fori_loop(2 * i, 2 * i + 2, gather_block, 0)
        at = pl.ds(pl.multiple_of(i * 16, 16), 16)
        for half in range(2):
            lanes = slice(half * 128, half * 128 + 128)
            total = None
            for pd in range(8):
                g = gtmp[half * 8 + pd]
                gscr[pd, at, lanes] = g.astype(BF)
                v = g * wexp[pd, at, lanes].astype(F32)
                total = v if total is None else total + v
            racc[half, at, :] = total
        return carry

    def keep(stage):
        at = pl.ds(pl.multiple_of(stage * STAGE * 16, 16), STAGE * 16)
        return pltpu.make_async_copy(gscr.at[:, at], g_ref.at[:, at], gsems.at[stage])

    def gather_stage(stage, carry):
        lax.fori_loop(stage * STAGE, (stage + 1) * STAGE, gather, 0)
        keep(stage).start()
        return carry

    lax.fori_loop(0, NB // 2 // STAGE, gather_stage, 0)
    for half in range(2):
        a = racc.at[half]
        lanes = slice(half * 128, half * 128 + 128)
        for k in range(2):
            at = slice(k * NB, (k + 1) * NB)
            first, second = (
                (a[pl.ds(2 * n, NB, 8), :] + a[pl.ds(2 * n + 1, NB, 8), :]).astype(BF) for n in (k, k + 2)
            )
            out_ref[at, lanes] = jnp.where(own == 0, first, second)
            send_ref[at, lanes] = jnp.where(own == 0, second, first)
    for stage in range(NB // 2 // STAGE):
        keep(stage).wait()


ANY = pl.BlockSpec(memory_space=pl.ANY)
SM = pl.BlockSpec(memory_space=pltpu.SMEM)
VM = pl.BlockSpec(memory_space=pltpu.VMEM)


def sampling_scratch(cells):
    return [
        pltpu.VMEM((2, cells, 2, D), BF),
        pltpu.VMEM((2, 2 * (cells + 2 * STRIDE), 128), F32),
        [[pltpu.VMEM((TABLE, 128), F32)] * 2] * 2,
        pltpu.VMEM((8, 2 * R, D), BF),
        pltpu.VMEM((2, 2 * R, 128), F32),
        pltpu.VMEM((2 * R, 128), F32),
        pltpu.VMEM((2, FR, 128), F32),
    ]


def sampling_semaphores():
    return [pltpu.SemaphoreType.DMA((2, COPIES)), pltpu.SemaphoreType.DMA(())]


def pick_scratch():
    return [pltpu.SMEM((NB,), jnp.int32)] * 128


def params(limit=VMEM_LIMIT):
    return pltpu.CompilerParams(vmem_limit_bytes=limit)


def cost(flops, moved):
    return pl.CostEstimate(flops=flops, bytes_accessed=moved, transcendentals=0)


def sample_forward(idx, size, ids, memory_t, s4, fa_mine, fa_other):
    frame = jax.ShapeDtypeStruct((FR, D), BF)
    return pl.pallas_call(
        forward_kernel,
        in_specs=[ANY, SM, SM, ANY, VM, VM, VM],
        out_specs=[ANY, VM, VM],
        out_shape=[jax.ShapeDtypeStruct((8, 2 * R, D), BF), frame, frame],
        scratch_shapes=sampling_scratch(1680)
        + [pltpu.VMEM((8, 2 * R, D), BF), pltpu.VMEM((16, 16, 128), F32)]
        + sampling_semaphores()
        + [pltpu.SemaphoreType.DMA((NB // 2 // STAGE,))]
        + pick_scratch(),
        compiler_params=params(),
        cost_estimate=cost(30_000_000_000, 60_000_000),
        name="sample_forward",
    )(idx, size, ids, memory_t, s4, fa_mine, fa_other)


def place_grads(ds, g2):
    ds = ds.astype(F32)
    for half in range(2):
        for k in range(4):
            piece = ds[k * NB : (k + 1) * NB, half * 128 : half * 128 + 128]
            for dx in range(2):
                g2[half, pl.ds(2 * k + dx, NB, 8), :] = piece


def coef_kernel(
    ids_ref, g_ref, ds_mine, ds_other, fa_mine, fa_other, out_ref, send_ref, g2, scr, dscr, fscr
):
    own = ids_ref[1]
    place_grads(join_frames(own, ds_mine, ds_other, dscr), g2)
    fa_all = join_frames(own, fa_mine, fa_other, fscr)
    fold = [fold_matrix(point) for point in range(4)]
    for dy in range(2):
        total = None
        for point in range(4):
            for half in range(2):
                lanes = slice(half * 128, half * 128 + 128)
                v = (g_ref[point * 2 + dy, :, lanes].astype(F32) * g2[half]).astype(BF)
                v = dot(v, fold[point][half * 128 : half * 128 + 128])
                total = v if total is None else total + v
        scr[dy] = total
    lane = lane_iota(NB)
    results = []
    for k in range(4):
        at = slice(k * NB, (k + 1) * NB)
        g = [[scr[dy, pl.ds(2 * k + dx, NB, 8), :] for dx in range(2)] for dy in range(2)]
        fa = fa_all[at]
        fx, fy, att = fa, pltpu.roll(fa, 96, 1), pltpu.roll(fa, 64, 1)
        top = (1.0 - fx) * g[0][0] + fx * g[0][1]
        bottom = (1.0 - fx) * g[1][0] + fx * g[1][1]
        d_att = (1.0 - fy) * top + fy * bottom
        d_fy = att * (bottom - top)
        d_fx = att * ((1.0 - fy) * (g[0][1] - g[0][0]) + fy * (g[1][1] - g[1][0]))
        gx = d_fx * fx * (1.0 - fx)
        gy = pltpu.roll(d_fy * fy * (1.0 - fy), 32, 1)
        weighted = pltpu.roll(att * d_att, 64, 1)
        res = jnp.where(lane < 32, gx, jnp.where(lane < 64, gy, jnp.where(lane < 96, weighted, 0.0)))
        results.append(res.astype(BF))
    for k in range(2):
        at = slice(k * NB, (k + 1) * NB)
        out_ref[at] = jnp.where(own == 0, results[k], results[k + 2])
        send_ref[at] = jnp.where(own == 0, results[k + 2], results[k])


def coef_backward(ids, gathered, ds_mine, ds_other, fa_mine, fa_other):
    frame = jax.ShapeDtypeStruct((FR, 128), BF)
    return pl.pallas_call(
        coef_kernel,
        in_specs=[SM] + [VM] * 5,
        out_specs=[VM, VM],
        out_shape=[frame, frame],
        scratch_shapes=[
            pltpu.VMEM((2, 2 * R, 128), F32),
            pltpu.VMEM((2, 2 * R, 128), F32),
            pltpu.VMEM((2, FR, D), BF),
            pltpu.VMEM((2, FR, 128), F32),
        ],
        compiler_params=params(32 * 1024 * 1024),
        cost_estimate=cost(2_000_000_000, 10_000_000),
        name="coef_backward",
    )(ids, gathered, ds_mine, ds_other, fa_mine, fa_other)


def scatter_kernel(
    idx_ref, size_ref, ids_ref, mem_ref, ds_mine, ds_other, fa_mine, fa_other,
    out_ref,
    buf, stage, tables, wexp, g2, cscr, fscr, dscr, sems, isem, sum_ref, *picks,
):
    own = ids_ref[1]
    chunks = Chunks(mem_ref, buf, stage, sems, size_ref, ids_ref)
    for copy in pick_copies(idx_ref, picks, isem):
        copy.start()
    chunks.start(0, 0)
    place_coefs(join_frames(own, fa_mine, fa_other, fscr), cscr)
    fill_weights(cscr, wexp)
    place_grads(join_frames(own, ds_mine, ds_other, dscr), g2)
    for pair in tables:
        for table in pair:
            table[:PAD, :] = jnp.zeros((PAD, 128), F32)
            table[TABLE - PAD :, :] = jnp.zeros((PAD, 128), F32)

    def clear(i, carry):
        for pair in tables:
            for table in pair:
                table[grid_row(i), :] = jnp.zeros((STRIDE, 128), F32)
        return carry

    lax.fori_loop(0, ROWS + 1, clear, 0)
    for copy in pick_copies(idx_ref, picks, isem):
        copy.wait()
    heads, rows = row_masks()

    def scatter(i, carry):
        at = pl.ds(pl.multiple_of(i * 16, 16), 16)
        for point in range(4):
            terms = [
                [wexp[point * 2 + dy, at, half * 128 : half * 128 + 128].astype(F32) * g2[half, at, :] for dy in range(2)]
                for half in range(2)
            ]
            for b in range(2):
                for low in range(2):
                    for half in range(2):
                        todo = []
                        for k in (low, low + 2):
                            for h in range(4):
                                r = picks[((half * 4 + h) * 4 + point) * 4 + k][2 * i + b] + (PAD - 2 * k)
                                table = tables[k // 2][half]
                                for dy in range(2):
                                    spot = pl.ds(r + dy * STRIDE, 8)
                                    value = table[spot, :] + terms[half][dy][8 * b : 8 * b + 8]
                                    todo.append((table, spot, value, heads[h] & rows[k]))
                        for table, spot, value, mask in todo:
                            pltpu.store(table.at[spot, :], value, mask=mask)
        return carry

    lax.fori_loop(0, NB // 2, scatter, 0)
    sum_ref[...] = jnp.zeros((D, D), F32)

    def reduce(j, m):
        for f in range(2):
            first = chunks.grid_rows(j * chunks.cells, f)
            last = chunks.grid_rows(jnp.minimum((j + 1) * chunks.cells, MCAP) - 1, f) + 1

            def copy_row(i, carry):
                at = grid_row(jnp.where(i < chunks.high[f], i, ROWS))
                for half in range(2):
                    stage[half, chunks.staged(i, f, j), :] = tables[f][half][at, :]
                return carry

            lax.fori_loop(first, last, copy_row, 0)
        if chunks.again:

            @pl.when(j == chunks.whole - 1)
            def _():
                stage[:, 2 * STRIDE : 2 * (STRIDE + chunks.again), :] = jnp.zeros((2, 2 * chunks.again, 128), F32)

        g = jnp.concatenate([stage[half, chunks.inner, :].astype(BF) for half in range(2)], 1)
        sum_ref[...] += dot_tn(m, g)

    chunks.run(reduce)
    for n in range(SHARDS):
        out_ref[ids_ref[2] ^ n] = sum_ref[n * RS : (n + 1) * RS].astype(BF)


def sample_backward(idx, size, ids, memory_t, ds_mine, ds_other, fa_mine, fa_other):
    return pl.pallas_call(
        scatter_kernel,
        in_specs=[ANY, SM, SM, ANY] + [VM] * 4,
        out_specs=VM,
        out_shape=jax.ShapeDtypeStruct((SHARDS, RS, D), BF),
        scratch_shapes=sampling_scratch(3344) + [pltpu.VMEM((2, FR, D), BF)] + sampling_semaphores() + [pltpu.VMEM((D, D), F32)] + pick_scratch(),
        compiler_params=params(),
        cost_estimate=cost(30_000_000_000, 60_000_000),
        name="sample_backward",
    )(idx, size, ids, memory_t, ds_mine, ds_other, fa_mine, fa_other)
EPSILON = 1e-05
SMOOTHING = 1e-06
SCALE = (D // H) ** (-0.5)
GELU_C = 0.7978845608028654
GELU_K = 0.044715


def norm_forward(y, gain, shift):
    centred = y - jnp.mean(y, -1, keepdims=True)
    rstd = lax.rsqrt(jnp.mean(centred * centred, -1, keepdims=True) + EPSILON)
    unit = centred * rstd
    return unit * gain + shift, unit, rstd


def norm_backward(grad, unit, rstd, gain):
    d_gain = jnp.sum(grad * unit, 0, keepdims=True)
    d_shift = jnp.sum(grad, 0, keepdims=True)
    g = grad * gain
    dy = rstd * (g - jnp.mean(g, -1, keepdims=True) - unit * jnp.mean(g * unit, -1, keepdims=True))
    return dy, d_gain, d_shift


def gelu_pair(u):
    sq = u * u
    t = jnp.tanh(GELU_C * (u + GELU_K * u * sq))
    half = 0.5 * (1.0 + t)
    slope = half + 0.5 * u * (1.0 - t * t) * (GELU_C * (1.0 + 3.0 * GELU_K * sq))
    return u * half, slope


def head_rows():
    lane = lax.broadcasted_iota(jnp.int32, (1, D), 1) // (D // H)
    return [(lane == h).astype(F32).astype(BF) for h in range(H)]


def attend_forward(x, wq, wk, wv, wo, bias, p_ref):
    xb = x.astype(BF)
    q, k, v = (dot(xb, w).astype(BF) for w in (wq, wk, wv))
    live = lax.broadcasted_iota(jnp.int32, (FR, FR), 1) < Q
    mixed = None
    for h, mask in enumerate(head_rows()):
        s = jnp.where(live, dot_nt(q * mask, k) * SCALE, -1e30)
        e = jnp.exp(s - jnp.max(s, -1, keepdims=True))
        weights = (e / jnp.sum(e, -1, keepdims=True)).astype(BF)
        p_ref[h] = weights
        part = dot(weights, v * mask)
        mixed = part if mixed is None else mixed + part
    mixed = mixed.astype(BF)
    return x + dot(mixed, wo) + bias, xb, q, k, v, mixed


def attend_backward(dy, xb, q, k, v, mixed, p_ref, wq, wk, wv, wo):
    dyb = dy.astype(BF)
    d_wo = dot_tn(mixed, dyb)
    d_mixed = dot_nt(dyb, wo).astype(BF)
    dq = dk = dv = None
    for h, mask in enumerate(head_rows()):
        weights = p_ref[h]
        dm = d_mixed * mask
        dp = dot_nt(dm, v)
        w32 = weights.astype(F32)
        prod = w32 * dp
        ds = ((prod - w32 * jnp.sum(prod, -1, keepdims=True)) * SCALE).astype(BF)
        parts = (dot(ds, k * mask), dot_tn(ds, q * mask), dot_tn(weights, dm))
        dq, dk, dv = parts if dq is None else (dq + parts[0], dk + parts[1], dv + parts[2])
    dq, dk, dv = dq.astype(BF), dk.astype(BF), dv.astype(BF)
    dx = dy + dot_nt(dq, wq) + dot_nt(dk, wk) + dot_nt(dv, wv)
    return dx, (dot_tn(xb, dq), dot_tn(xb, dk), dot_tn(xb, dv), d_wo)


def group_spread(x, op):
    lane = lane_iota(x.shape[0])
    x = op(x, pltpu.roll(x, 64, 1))
    x = op(x, pltpu.roll(x, 32, 1))
    for step in (1, 2):
        other = jnp.where((lane & step) == 0, pltpu.roll(x, 128 - step, 1), pltpu.roll(x, step, 1))
        x = op(x, other)
    return x


def order(bits):
    return [sum(bit for i, bit in enumerate(bits) if n >> i & 1) for n in range(SHARDS)]


def unpack_early(me, own, mine_ref, other_ref, w_ref, wq_ref, s4_ref, vec_ref):
    def take(first_ref, second_ref):
        rows = jnp.zeros((24, D), F32)
        for n in range(SHARDS):
            at = pl.ds(pl.multiple_of((me ^ order(EARLY_BITS)[n]) * RS, RS), RS)
            for m in range(4):
                w_ref[m, at, :] = first_ref[n, m * RS : (m + 1) * RS]
            s4_ref[at, :] = second_ref[n, :RS]
            wq_ref[at, :D] = second_ref[n, RS : 2 * RS]
            right = second_ref[n, 2 * RS : 2 * RS + RS // 2]
            wq_ref[at, D:] = jnp.concatenate([right[:, :128], right[:, 128:]], 0)
            rows = rows + second_ref[n, 2 * RS + RS // 2 : 128].astype(F32)[:24]
        vec_ref[...] = rows

    @pl.when(own == 0)
    def _():
        take(mine_ref, other_ref)

    @pl.when(own == 1)
    def _():
        take(other_ref, mine_ref)


def front_kernel(
    ids_ref, x_ref, mine_ref, other_ref,
    w_ref, wq_ref, s4_ref, vec_ref, total_ref, dec_ref, y_ref, q_ref, k_ref, v_ref, m_ref, p_ref, fa_ref, send_ref, att_ref,
):
    unpack_early(ids_ref[2], ids_ref[1], mine_ref, other_ref, w_ref, wq_ref, s4_ref, vec_ref)
    total_ref[...] = jnp.sum(vec_ref[21:22], -1, keepdims=True) / RS
    x = jnp.concatenate([x_ref[...].astype(F32), jnp.zeros((FR - Q, D), F32)], 0)
    y, _, q, k, v, mixed = attend_forward(x, w_ref[0], w_ref[1], w_ref[2], w_ref[3], vec_ref[10:11], p_ref)
    y_ref[...], q_ref[...], k_ref[...], v_ref[...], m_ref[...] = y, q, k, v, mixed
    dec, _, _ = norm_forward(y, vec_ref[0:1], vec_ref[1:2])
    dec_ref[...] = dec
    proj = dot(dec.astype(BF), wq_ref[...])
    fx, fy = jax.nn.sigmoid(proj[:, :128]), jax.nn.sigmoid(proj[:, 128:256])
    logits = proj[:, 256:]
    e = jnp.exp(logits - group_spread(logits, jnp.maximum))
    att = e / group_spread(e, jnp.add)
    att_ref[...] = att
    lane = lane_iota(FR)
    for out, back in ((fa_ref, ids_ref[0] * 32), (send_ref, (ids_ref[0] ^ 1) * 32)):
        out[...] = jnp.where(
            lane < 32,
            pltpu.roll(fx, 128 - back, 1),
            jnp.where(lane < 64, pltpu.roll(fy, 160 - back, 1), pltpu.roll(att, 192 - back, 1)),
        )


def frame_rows(dt, width=D):
    return jax.ShapeDtypeStruct((FR, width), dt)


WEIGHT_SHAPES = [
    jax.ShapeDtypeStruct((4, D, D), BF),
    jax.ShapeDtypeStruct((D, 384), BF),
    jax.ShapeDtypeStruct((D, D), BF),
    jax.ShapeDtypeStruct((24, D), F32),
    jax.ShapeDtypeStruct((1, 1), F32),
]
DENSE_LIMIT = 40 * 1024 * 1024


def front_forward(ids, x, mine, other):
    return pl.pallas_call(
        front_kernel,
        in_specs=[SM, VM, VM, VM],
        out_specs=[VM] * 15,
        out_shape=WEIGHT_SHAPES
        + [frame_rows(F32)] * 2
        + [frame_rows(BF)] * 4
        + [jax.ShapeDtypeStruct((H, FR, FR), BF)]
        + [frame_rows(F32, 128)] * 3,
        compiler_params=params(),
        cost_estimate=cost(1_000_000_000, 5_000_000),
        name="front_forward",
    )(ids, x, mine, other)


def front_back_kernel(
    ids_ref, near_ref, far_ref, att_ref, dres_ref, x_ref, dec_ref, y_ref, q_ref, k_ref, v_ref, m_ref, p_ref,
    w_ref, wq_ref, vec_ref, dpost_ref,
    mine_ref, send_ref, all_ref,
):
    me, own, level = ids_ref[2], ids_ref[1], ids_ref[0]
    lane = lane_iota(FR)
    cols = [None, None, None]
    for n, gp_ref in enumerate((near_ref.at[0], near_ref.at[1], far_ref.at[0], far_ref.at[1])):
        at = level ^ n
        gp = gp_ref[...].astype(F32)
        here = lane // 32 == at
        for part in range(3):
            piece = jnp.where(here, pltpu.roll(gp, (at + 4 - part) % 4 * 32, 1), 0.0)
            cols[part] = piece if cols[part] is None else cols[part] + piece
    weighted = cols[2]
    cols[2] = weighted - att_ref[...] * group_spread(weighted, jnp.add)
    grad = jnp.concatenate([c.astype(BF) for c in cols], 1)
    d_dec = dres_ref[...] + dot_nt(grad, wq_ref[...])
    _, unit, rstd = norm_forward(y_ref[...], vec_ref[0:1], vec_ref[1:2])
    dy, d_gain, d_shift = norm_backward(d_dec, unit, rstd, vec_ref[0:1])
    xb = jnp.concatenate([x_ref[...].astype(F32), jnp.zeros((FR - Q, D), F32)], 0).astype(BF)
    _, d_w = attend_backward(
        dy, xb, q_ref[...], k_ref[...], v_ref[...], m_ref[...], p_ref, w_ref[0], w_ref[1], w_ref[2], w_ref[3]
    )
    d_wq = dot_tn(dec_ref[...].astype(BF), grad)
    front = jnp.concatenate([d_gain, d_shift, jnp.zeros((8, D), F32), jnp.sum(dy, 0, keepdims=True), jnp.zeros((13, D), F32)], 0)
    d_vec = dpost_ref[...] + front
    d_w = [w.astype(BF) for w in d_w]
    d_wq = d_wq.astype(BF)
    d_vec = d_vec.astype(BF)
    first, second = own, 1 - own
    for shard in range(SHARDS):
        n = me ^ shard
        at = slice(shard * RS, (shard + 1) * RS)
        for m in range(4):
            all_ref[first, n, m * RS : (m + 1) * RS] = d_w[m][at]
        all_ref[second, n, :RS] = jnp.zeros((RS, D), BF)
        all_ref[second, n, RS : 2 * RS] = d_wq[at, :D]
        right = d_wq[at, D:]
        all_ref[second, n, 2 * RS : 2 * RS + RS // 2] = jnp.concatenate([right[: RS // 2], right[RS // 2 :]], 1)
        all_ref[second, n, 2 * RS + RS // 2 : 128] = jnp.concatenate([d_vec, jnp.zeros((24, D), BF)], 0)
    mine_ref[...] = all_ref[0]
    send_ref[...] = all_ref[1]


def front_backward(*args):
    half = jax.ShapeDtypeStruct((SHARDS, 128, D), BF)
    return pl.pallas_call(
        front_back_kernel,
        in_specs=[SM] + [VM] * 16,
        out_specs=[VM, VM],
        out_shape=[half, half],
        scratch_shapes=[pltpu.VMEM((2, SHARDS, 128, D), BF)],
        compiler_params=params(),
        cost_estimate=cost(2_000_000_000, 5_000_000),
        name="front_backward",
    )(*args)


def smooth_max(a, b):
    return 0.5 * (a + b + jnp.sqrt((a - b) * (a - b) + SMOOTHING))


def smooth_min(a, b):
    return 0.5 * (a + b - jnp.sqrt((a - b) * (a - b) + SMOOTHING))


def box_cost(p, t):
    distance = sum(jnp.sqrt((a - b) * (a - b) + 0.01) for a, b in zip(p, t))
    inter = hull = None
    for axis in range(2):
        p_low, p_up = p[axis] - 0.5 * p[axis + 2], p[axis] + 0.5 * p[axis + 2]
        t_low, t_up = t[axis] - 0.5 * t[axis + 2], t[axis] + 0.5 * t[axis + 2]
        over = smooth_max(smooth_min(p_up, t_up) - smooth_max(p_low, t_low), 0.0)
        enclose = smooth_max(p_up, t_up) - smooth_min(p_low, t_low)
        inter, hull = (over, enclose) if inter is None else (inter * over, hull * enclose)
    union = p[2] * p[3] + t[2] * t[3] - inter
    general = inter / union - (hull - union) / hull
    return 5.0 * distance + 2.0 * (1.0 - general)


LOSS_UNITS = [16.0 ** (3 - n) for n in range(8)]
LATE = 23 * RS // 2


def unpack_late(me, own, mine, other, ws_ref, fi_ref, fo_ref):
    def take(halves):
        for n in range(SHARDS):
            shard = me ^ order(LATE_BITS)[n]
            at = pl.ds(pl.multiple_of(shard * RS, RS), RS)

            def rows(block):
                parts = []
                for p in (block * RS, block * RS + RS // 2):
                    parts.append(halves[p // LATE][n // 4][n % 4, p % LATE : p % LATE + RS // 2])
                return jnp.concatenate(parts, 0)

            for m in range(7):
                ws_ref[m, at] = rows(m)
            for i in range(2):
                for c in range(4):
                    fi_ref[i, at, c * D : (c + 1) * D] = rows(7 + 4 * i + c)
                    down = pl.ds(pl.multiple_of((4 * shard + c) * RS, RS), RS)
                    fo_ref[i, down] = rows(15 + 4 * i + c)

    @pl.when(own == 0)
    def _():
        take((mine, other))

    @pl.when(own == 1)
    def _():
        take((other, mine))


def post_kernel(
    ids_ref, match_ref, count_ref, s_ref, add_ref, dec_ref, tgt_ref, late_a, late_b, late_c, late_d, vec_ref,
    ds_ref, dres_ref, mine_ref, send_ref, dvec_ref,
    ws_ref, fi_ref, fo_ref, all_ref, p_ref, box_ref, pick_ref,
):
    own = ids_ref[1]
    f = own
    me = ids_ref[2]
    unpack_late(me, own, (late_a, late_b), (late_c, late_d), ws_ref, fi_ref, fo_ref)
    dvec_ref[...] = jnp.zeros_like(dvec_ref)
    kept, given = own, 1 - own

    def put_square(m, grad):
        grad = grad.astype(BF)
        for n in range(SHARDS):
            all_ref[kept, me ^ n, m * RS : (m + 1) * RS] = grad[n * RS : (n + 1) * RS]

    def put_in(i, grad):
        grad = grad.astype(BF)
        for n in range(SHARDS):
            for c in range(4):
                piece = grad[n * RS : (n + 1) * RS, c * D : (c + 1) * D]
                if i == 0:
                    all_ref[kept, me ^ n, (7 + c) * RS : (8 + c) * RS] = piece
                else:
                    all_ref[given, me ^ n, c * RS : (c + 1) * RS] = piece

    def put_out(i, grad):
        grad = grad.astype(BF)
        for n in range(SHARDS):
            all_ref[given, me ^ n, (4 + 4 * i) * RS : (8 + 4 * i) * RS] = grad[n * 4 * RS : (n + 1) * 4 * RS]

    vec = lambda row: vec_ref[row : row + 1]
    total = lambda value: jnp.sum(value, 0, keepdims=True)

    def add_vec(row, value):
        dvec_ref[row : row + 1] += value

    sb = (s_ref[...].astype(F32) + add_ref[...].astype(F32)).astype(BF)
    first, unit2, rstd2 = norm_forward(dec_ref[...] + dot(sb, ws_ref[0]) + vec(11), vec(2), vec(3))
    firstb = first.astype(BF)
    hid1, slope1 = gelu_pair(dot(firstb, fi_ref[0]))
    hid1 = hid1.astype(BF)
    second, unit3, rstd3 = norm_forward(first + dot(hid1, fo_ref[0]) + vec(12), vec(4), vec(5))
    y4, secondb, q, k, v, mixed = attend_forward(second, ws_ref[1], ws_ref[2], ws_ref[3], ws_ref[4], vec(13), p_ref)
    third, unit4, rstd4 = norm_forward(y4, vec(6), vec(7))
    thirdb = third.astype(BF)
    hid2, slope2 = gelu_pair(dot(thirdb, fi_ref[1]))
    hid2 = hid2.astype(BF)
    fourth, unit5, rstd5 = norm_forward(third + dot(hid2, fo_ref[1]) + vec(14), vec(8), vec(9))
    fourthb = fourth.astype(BF)
    z1, slope_z1 = gelu_pair(dot(fourthb, ws_ref[5]) + vec(15))
    z1 = z1.astype(BF)
    z2, slope_z2 = gelu_pair(dot(z1, ws_ref[6]) + vec(16))
    z2 = z2.astype(BF)
    w3 = jnp.concatenate([vec_ref[17:21], jnp.zeros((124, D), F32)], 0).astype(BF)
    boxes = jax.nn.sigmoid(dot_nt(z2, w3))
    box_ref[...] = boxes
    slots = tgt_ref.shape[1]
    for o in range(slots):
        pick_ref[o : o + 1, :] = box_ref[pl.ds(match_ref[f, o], 1), :]
    picked = pick_ref[...]
    pred = [picked[:, c : c + 1] for c in range(4)]
    target = [tgt_ref[own, :, c : c + 1] for c in range(4)]
    valid = (lax.broadcasted_iota(jnp.int32, (slots, 1), 0) < count_ref[f]).astype(F32)
    price, pull = jax.vjp(lambda *p: box_cost(p, target), *pred)
    loss = jnp.sum(valid * price, 0, keepdims=True)
    count = jnp.sum(vec_ref[21:22], -1, keepdims=True) / RS
    d_pred = pull(valid / count)
    lane = lane_iota(slots)
    rows = jnp.zeros((slots, 128), F32)
    for c in range(4):
        rows = jnp.where(lane == c, d_pred[c], rows)
    pick_ref[...] = rows
    box_ref[...] = jnp.zeros((FR, 128), F32)
    for o in range(slots):
        box_ref[pl.ds(match_ref[f, o], 1), :] = pick_ref[o : o + 1, :]
    d_logit = (box_ref[...] * boxes * (1.0 - boxes)).astype(BF)
    dvec_ref[17:21] += dot_tn(d_logit, z2)[0:4]
    du = dot(d_logit, w3) * slope_z2
    add_vec(16, total(du))
    du = du.astype(BF)
    put_square(6, dot_tn(z1, du))
    du = dot_nt(du, ws_ref[6]) * slope_z1
    add_vec(15, total(du))
    du = du.astype(BF)
    put_square(5, dot_tn(fourthb, du))
    grad = dot_nt(du, ws_ref[5])

    def ffn_back(grad, unit, rstd, i, row, bias, hid, slope, inputb):
        dy, d_gain, d_shift = norm_backward(grad, unit, rstd, vec(row))
        add_vec(row, d_gain)
        add_vec(row + 1, d_shift)
        add_vec(bias, total(dy))
        dyb = dy.astype(BF)
        put_out(i, dot_tn(hid, dyb))
        du = (dot_nt(dyb, fo_ref[i]) * slope).astype(BF)
        put_in(i, dot_tn(inputb, du))
        return dy + dot_nt(du, fi_ref[i])

    grad = ffn_back(grad, unit5, rstd5, 1, 8, 14, hid2, slope2, thirdb)
    dy, d_gain, d_shift = norm_backward(grad, unit4, rstd4, vec(6))
    add_vec(6, d_gain)
    add_vec(7, d_shift)
    add_vec(13, total(dy))
    grad, d_w = attend_backward(dy, secondb, q, k, v, mixed, p_ref, ws_ref[1], ws_ref[2], ws_ref[3], ws_ref[4])
    for i in range(4):
        put_square(1 + i, d_w[i])
    grad = ffn_back(grad, unit3, rstd3, 0, 4, 12, hid1, slope1, firstb)
    dy, d_gain, d_shift = norm_backward(grad, unit2, rstd2, vec(2))
    add_vec(2, d_gain)
    add_vec(3, d_shift)
    add_vec(11, total(dy))
    dres_ref[...] = dy
    dyb = dy.astype(BF)
    put_square(0, dot_tn(sb, dyb))
    ds_ref[...] = dot_nt(dyb, ws_ref[0]).astype(BF)
    row = lax.broadcasted_iota(jnp.int32, (RS, D), 0)
    rows, above = jnp.zeros((RS, D), F32), jnp.zeros((1, 1), F32)
    for n, unit in enumerate(LOSS_UNITS):
        whole = jnp.floor(loss * (1.0 / unit))
        rows = jnp.where(row == n, whole - 16.0 * above, rows)
        above = whole
    rows = rows.astype(BF)
    for n in range(SHARDS):
        all_ref[kept, me ^ n, 11 * RS : 12 * RS] = rows
    mine_ref[...] = all_ref[0]
    send_ref[...] = all_ref[1]


def post_step(ids, match, count, half, add, dec, target, late, vec):
    half_rows = jax.ShapeDtypeStruct((SHARDS, 12 * RS, D), BF)
    return pl.pallas_call(
        post_kernel,
        in_specs=[SM, SM, SM] + [VM] * 9,
        out_specs=[VM] * 5,
        out_shape=[frame_rows(BF), frame_rows(F32), half_rows, half_rows, jax.ShapeDtypeStruct((24, D), F32)],
        scratch_shapes=[
            pltpu.VMEM((7, D, D), BF),
            pltpu.VMEM((2, D, 4 * D), BF),
            pltpu.VMEM((2, 4 * D, D), BF),
            pltpu.VMEM((2, SHARDS, 12 * RS, D), BF),
            pltpu.VMEM((H, FR, FR), BF),
            pltpu.VMEM((FR, 128), F32),
            pltpu.VMEM((target.shape[1], 128), F32),
        ],
        compiler_params=params(DENSE_LIMIT),
        cost_estimate=cost(8_000_000_000, 10_000_000),
        name="post_step",
    )(ids, match, count, half, add, dec, target, *late, vec)


LEARNING_RATE = 2.0
MOMENTUM = 0.5
AVERAGING = 0.5


def update(master, gradient, moment, average):
    moment_new = MOMENTUM * moment + gradient
    master_new = master - LEARNING_RATE * (gradient + MOMENTUM * moment_new)
    average_new = AVERAGING * average + (1.0 - AVERAGING) * master_new
    return (master_new, master_new.astype(BF), moment_new, average_new)


def apply_kernel(ids_ref, last_mine, last_other, late_mine, late_other, *refs):
    own, me = ids_ref[1], ids_ref[2]
    masters, moments, averages, loss_ref, outs = refs[:5], refs[5:10], refs[10:15], refs[15], refs[16:]

    def halves(mine, other):
        mine, other = mine[...], other[...]
        return jnp.where(own == 0, mine, other), jnp.where(own == 0, other, mine)

    last, late = halves(last_mine, last_other), halves(late_mine, late_other)

    def step(which, index, grad):
        new = update(masters[which][index], grad, moments[which][index], averages[which][index])
        for out, value in zip(outs[4 * which : 4 * which + 4], new):
            out[index] = value

    def block(rows, n, count=1):
        return rows[n * RS : (n + count) * RS]

    step(0, (slice(None), slice(0, D)), block(last[1], 1))
    right = last[1][2 * RS : 2 * RS + RS // 2]
    step(0, (slice(0, RS // 2), slice(D, D + 128)), right[:, :128])
    step(0, (slice(RS // 2, RS), slice(D, D + 128)), right[:, 128:])
    for m in range(12):
        step(1, (m,), block(last[0], m) if m < 4 else block(last[1], 0) if m == 4 else block(late[0], m - 5))
    for i in range(2):
        for c in range(4):
            step(2, (i, slice(None), slice(c * D, (c + 1) * D)), block(late[1], c) if i else block(late[0], 7 + c))
        step(3, (i,), block(late[1], 4 + 4 * i, 4))
    vec = last[1][2 * RS + RS // 2 : 2 * RS + RS // 2 + 24]
    vec = jnp.where(me >= 4, vec[:, 128:], vec[:, :128])
    vec = pltpu.roll(vec, (4 - me % 4) % 4 * RS, 1)
    step(4, (slice(None), slice(None)), vec[:21, :RS])
    loss_ref[...] = sum(late[0][11 * RS + n : 11 * RS + n + 1, 0:1] * unit for n, unit in enumerate(LOSS_UNITS))


def apply_updates(ids, grads, masters, moments, averages):
    shapes = [jax.ShapeDtypeStruct((1, 1), F32)]
    for master in masters:
        full = jax.ShapeDtypeStruct(master.shape, F32)
        shapes += [full, jax.ShapeDtypeStruct(master.shape, BF), full, full]
    loss, *outs = pl.pallas_call(
        apply_kernel,
        in_specs=[SM] + [VM] * 19,
        out_specs=[VM] * 21,
        out_shape=shapes,
        compiler_params=params(24 * 1024 * 1024),
        cost_estimate=cost(3_000_000, 8_000_000),
        name="apply_updates",
    )(ids, *grads, *masters, *moments, *averages)
    return loss.reshape(()), outs


def pairs(size, bit):
    return [(i, i ^ bit) for i in range(size)]


def swap_core(value):
    return lax.ppermute(value, "level", pairs(4, 1))


def swap_chip(value):
    return lax.ppermute(value, "level", pairs(4, 2))


def pick(pair, index):
    return lax.dynamic_index_in_dim(pair, index, 0, keepdims=False)


def in_order(mine, other, index):
    return jnp.where(index == 0, mine, other), jnp.where(index == 0, other, mine)


def early_rows(square, query, vec):
    right = jnp.concatenate([query[: RS // 2, D:], query[RS // 2 :, D:]], 1)
    second = jnp.concatenate([square[4], query[:, :D], right, vec, jnp.zeros((24, D), vec.dtype)], 0)
    return jnp.stack([square[:4].reshape(4 * RS, D), second])


def late_rows(square, ffn_in, ffn_out):
    return jnp.concatenate(
        [
            square.reshape(7 * RS, D),
            ffn_in.reshape(2, RS, 4, D).transpose(0, 2, 1, 3).reshape(8 * RS, D),
            ffn_out.reshape(8 * RS, D),
        ],
        0,
    )


def gather_weights(dp, own, rows, w_query, w_square, w_ffn_in, w_ffn_out, vectors, count):
    rs = D // dp
    shard = lax.axis_index("dp")
    here = jnp.arange(D, dtype=jnp.int32)[None, :] // rs == shard
    vec = jnp.where(here, jnp.tile(jnp.pad(vectors, ((0, 3), (0, 0))), (1, dp)), 0.0)
    vec = jnp.where(here & (jnp.arange(24)[:, None] == 21), count, vec)
    if dp == SHARDS:
        early = pick(early_rows(w_square[:5], w_query, vec).astype(BF), own)[None]
        first = lax.ppermute(early, "dp", pairs(dp, EARLY_BITS[0]))
        early, first, *late = lax.optimization_barrier((early, first, w_square[5:], w_ffn_in, w_ffn_out))
        late = pick(late_rows(*(w.astype(BF) for w in late)).reshape(2, -1, D), own)[None]
        early, late, rows = lax.optimization_barrier((jnp.concatenate([early, first], 0), late, rows))
        second = lax.ppermute(early, "dp", pairs(dp, EARLY_BITS[1]))
        late_first = lax.ppermute(late, "dp", pairs(dp, LATE_BITS[0]))
        early = jnp.concatenate([early, second], 0)
        late = jnp.concatenate([late, late_first], 0)
        early, late = lax.optimization_barrier((early, late))
        third = lax.ppermute(early, "dp", pairs(dp, EARLY_BITS[2]))
        late = (late, lax.ppermute(late, "dp", pairs(dp, LATE_BITS[1])))
        early = jnp.concatenate([early, third], 0)
        return rows, early, swap_core(early), late

    def whole(weight, dim):
        return lax.all_gather(weight.astype(BF), "dp", axis=dim, tiled=True)

    square, query = whole(w_square, 1), whole(w_query, 0)
    ffn_in, ffn_out = whole(w_ffn_in, 1), whole(w_ffn_out, 1)
    vec = lax.psum(vec, "dp")
    early, late = [], []
    for n in order(EARLY_BITS):
        at = slice(n * RS, (n + 1) * RS)
        columns = jnp.where(jnp.arange(D)[None, :] // RS == n, vec, 0.0).astype(BF)
        early.append(early_rows(square[:5, at], query[at], columns))
    for n in order(LATE_BITS):
        at = slice(n * RS, (n + 1) * RS)
        late.append(late_rows(square[5:, at], ffn_in[:, at], ffn_out[:, 4 * n * RS : 4 * (n + 1) * RS]))
    early = jnp.stack(early, 1)
    late = pick(jnp.stack(late).reshape(SHARDS, 2, -1, D).transpose(1, 0, 2, 3), own).reshape(2, 4, -1, D)
    return rows, pick(early, own), pick(early, 1 - own), late


def halve(value):
    value = value.reshape(-1, 2, *value.shape[1:])
    return value[:, 0], value[:, 1].astype(BF)


def send(value, bit):
    return lax.ppermute(value, "dp", pairs(SHARDS, bit)).astype(F32)


def after(value, event):
    return lax.optimization_barrier((value, event))[0]


def shards(
    queries, memory, frame_size, sample_pick, target_box, match, obj_count,
    w_query, w_square, w_ffn_in, w_ffn_out, vectors,
    m_query, m_square, m_ffn_in, m_ffn_out, m_vectors,
    a_query, a_square, a_ffn_in, a_ffn_out, a_vectors,
):
    dp = lax.axis_size("dp")
    rs = D // dp
    shard = lax.axis_index("dp")
    level = lax.axis_index("level")
    own = level % 2
    me = shard if dp == SHARDS else 0
    ids = jnp.stack([level, own, me, 0]).astype(jnp.int32)
    rows = pick_rows(frame_size, ids, sample_pick[:, 0, :].T)
    rows, mine, other, late = gather_weights(
        dp, own, rows, w_query, w_square, w_ffn_in, w_ffn_out, vectors, jnp.sum(obj_count).astype(F32)
    )
    memory_t = memory.transpose(1, 2, 0, 3)
    x = pick(queries.reshape(2, Q, D), own)
    w4, wq, s4, vec, total, dec, y, q, k, v, mixed, p, fa, fa_send, att = front_forward(ids, x, mine, other)
    fa_other = swap_core(fa_send)
    if dp == SHARDS:
        late = jnp.concatenate([late[0], after(late[1], att)], 0)
        s4 = after(s4, late)
        late = (late, lax.ppermute(late, "dp", pairs(dp, LATE_BITS[2])))
    gathered, part, part_send = sample_forward(rows, frame_size, ids, memory_t, s4, fa, fa_other)
    part_other = swap_core(part_send)
    half = (part.astype(F32) + part_other.astype(F32)).astype(BF)
    half_other = swap_chip(half)
    late_end = after(late[1], part_other)
    late = (late[0], late_end, swap_core(late[0]), swap_core(late_end))
    ds, dres, late_mine, late_send, dvec = post_step(
        ids, match, obj_count, half, half_other, dec, target_box, late, vec
    )
    ds_other = swap_core(ds)
    late_sent = swap_core(after(late_send, ds_other))
    gp, gp_send = coef_backward(ids, gathered, ds, ds_other, fa, fa_other)
    near = jnp.stack([gp, swap_core(gp_send)])
    far = swap_chip(near)
    late_sum = late_mine.astype(F32) + late_sent.astype(F32)
    late_kept, late_out = halve(late_sum)
    near, late_out, ds_other = lax.optimization_barrier((near, late_out, ds_other))
    if dp == SHARDS:
        late_in = send(late_out, 1)
    d_s4 = sample_backward(rows, frame_size, ids, memory_t, ds, ds_other, fa, fa_other)
    d_s4_other = swap_chip(d_s4)
    if dp == SHARDS:
        late_kept, late_out = halve(late_kept + after(late_in, d_s4))
        near, late_out = lax.optimization_barrier((near, late_out))
        late_in = send(late_out, 2)
    last_mine, last_send = front_backward(
        ids, near, far, att, dres, x, dec, y, q, k, v, mixed, p, w4, wq, vec, dvec
    )
    d_s4 = (d_s4.astype(F32) + d_s4_other.astype(F32)).astype(BF)
    d_s4 = d_s4.astype(F32) + swap_core(d_s4).astype(F32)
    last_sent = swap_core(last_send)
    d_s4 = jnp.pad(jnp.where(own == 1, d_s4, 0.0), ((0, 0), (0, 128 - RS), (0, 0)))
    last = last_mine.astype(F32) + last_sent.astype(F32) + d_s4
    if dp == SHARDS:
        late_kept, late_out = halve(late_kept + after(late_in, last_sent))
        last, late_out = lax.optimization_barrier((last, late_out))
        late_in = send(late_out, 4)
        for bit in (1, 2, 4):
            last_kept, last_out = halve(last)
            last = last_kept + send(last_out, bit)
        late_sum = (late_kept + after(late_in, last))[0]
        last = last[0]
    masters = (w_query, w_square, w_ffn_in, w_ffn_out, vectors)
    moments = (m_query, m_square, m_ffn_in, m_ffn_out, m_vectors)
    averages = (a_query, a_square, a_ffn_in, a_ffn_out, a_vectors)
    last_other, late_other = swap_core(last), swap_core(late_sum)
    if dp == SHARDS:
        loss, outs = apply_updates(ids, (last, last_other, late_sum, late_other), masters, moments, averages)
    else:
        last, late = in_order(last, last_other, own), in_order(late_sum, late_other, own)
        loss = lax.psum(late[0][0, 11 * RS : 11 * RS + 8, 0], "dp")

        def square(rows):
            return rows.reshape(SHARDS, -1, RS, D).transpose(1, 0, 2, 3).reshape(-1, D, D)

        right = last[1][:, 2 * RS : 2 * RS + RS // 2].reshape(SHARDS, RS // 2, 2, 128).transpose(0, 2, 1, 3)
        g_query = jnp.concatenate([square(last[1][:, RS : 2 * RS])[0], right.reshape(D, 128)], 1)
        g_vec = last[1][0, 2 * RS + RS // 2 : 2 * RS + RS // 2 + 21]
        g_square = jnp.concatenate([square(last[0]), square(last[1][:, :RS]), square(late[0][:, : 7 * RS])], 0)
        g_in = [x.reshape(SHARDS, 4, RS, D).transpose(0, 2, 1, 3) for x in (late[0][:, 7 * RS : 11 * RS], late[1][:, : 4 * RS])]
        g_in = jnp.concatenate([x.reshape(1, D, 4 * D) for x in g_in], 0)
        g_out = late[1][:, 4 * RS :].reshape(SHARDS, 2, 4 * RS, D).transpose(1, 0, 2, 3).reshape(2, 4 * D, D)

        def scatter(grad, dim):
            return lax.psum_scatter(grad, "dp", scatter_dimension=dim, tiled=True)

        g_query, g_square, g_vec = scatter(g_query, 0), scatter(g_square, 1), scatter(g_vec, 1)
        g_in, g_out = scatter(g_in, 1), scatter(g_out, 1)
        grads = (g_query, g_square, g_in, g_out, g_vec)
        outs = [out for group in zip(masters, grads, moments, averages) for out in update(*group)]
        loss = jnp.sum(loss * jnp.array(LOSS_UNITS, F32))
    return (loss, total.reshape(()), *outs)


def solution(mesh):
    rows, mid, low = P("dp", None), P(None, "dp", None), P(None, "dp")
    five = (rows, mid, mid, mid, low)
    return jax.shard_map(
        shards,
        mesh=mesh,
        in_specs=(
            rows,
            P("dp", "level", None, None),
            rows,
            P("dp", "level", None),
            P("dp", None, None),
            rows,
            P("dp"),
        )
        + five * 3,
        out_specs=(P(), P()) + tuple(spec for spec in five for _ in range(4)),
        check_vma=False,
    )
```

time: 3860 us -> 195 us (0.05)
  matrix products: 2720 us -> 0 us
  local copies, waits for them, and re-layouts: 423 us -> 10.3 us
  waiting for transfers between devices: 441 us -> 42.2 us
  blocking collectives: 146 us -> 0 us
  Pallas kernels: 0 us -> 104 us
  other arithmetic: 71.2 us -> 12.2 us
    dot_general x110 -> x0, matrix products: 2710 us -> none  [the longest x16 990 us: sample_forward(): jnp.dot(sampling_matrix(cell_row, coef_row), table.astype(jnp.float32), p...]
    reduce_scatter x4 -> x0, waiting for transfers between devices: 274 us -> none  [the longest x1 75.5 us: shards(): lax.psum_scatter(totals[1], 'dp', scatter_dimension=1, tiled=True)]
    pallas_call x0 -> x8, Pallas kernels: none -> 104 us  [the longest x1 32.1 us: sample_backward(): pl.pallas_call(scatter_kernel, in_specs=[ANY, SM, SM, ANY] + [VM] * 4, ou...]
    convert_element_type x17 -> x6, local copies, waits for them, and re-layouts: 97 us -> 0.19 us  [halve(): return (value[:, 0], value[:, 1].astype(BF))]
    squeeze x12 -> x1, local copies, waits for them, and re-layouts: 94.5 us -> 0.68 us  [pick(): return lax.dynamic_index_in_dim(pair, index, 0, keepdims=False)]
    psum x4 -> x0, blocking collectives: 82.6 us -> none  [the longest x1 39.5 us: shards(): loss_sum = lax.psum(loss_local * keep_share, ('dp', 'level'))]
    all_gather x3 -> x0, waiting for transfers between devices: 78.8 us -> none  [the longest x1 41 us: shards(): lax.all_gather(w_ffn_in.astype(jnp.bfloat16), 'dp', axis=1, tiled=True)]
    psum x3 -> x0, waiting for transfers between devices: 72.6 us -> none  [the longest x1 67.4 us: shards(): lax.psum(grad_query.astype(jnp.bfloat16), 'level').astype(jnp.float32)]
  transfers between devices with their start and end apart: 11 -> 27, of which waited for: 9 -> 16; matrix products, arithmetic and copies ran while one was open for 4% -> 6% of each run, Pallas kernels for 0% -> 43%
where the time goes in v1:
time: 195 us; the launch traced here: 194 us
  Pallas kernels  104 us (53%)
  waiting for transfers between devices  42.2 us (22%)
  starting transfers between devices  22.7 us (12%)
  other arithmetic  12.2 us (6%)
  local copies, waits for them, and re-layouts  10.3 us (5%)
  between operations  2.33 us (1%)
    pallas_call x1, Pallas kernels, sample_backward(): pl.pallas_call(scatter_kernel, in_specs=[ANY, SM, SM, ANY] + [VM] * 4, ou...  32.1 us
    pallas_call x1, Pallas kernels, sample_forward(): pl.pallas_call(forward_kernel, in_specs=[ANY, SM, SM, ANY, VM, VM, VM], o...  31.2 us
    ppermute x6, waiting for transfers between devices, send(): return lax.ppermute(value, 'dp', pairs(SHARDS, bit)).astype(F32)  19.9 us
    pallas_call x1, Pallas kernels, post_step(): pl.pallas_call(post_kernel, in_specs=[SM, SM, SM] + [VM] * 9, out_specs=[...  17.4 us
    pallas_call x1, Pallas kernels, front_backward(): pl.pallas_call(front_back_kernel, in_specs=[SM] + [VM] * 16, out_specs=[V...  9.7 us
    pallas_call x1, Pallas kernels, front_forward(): pl.pallas_call(front_kernel, in_specs=[SM, VM, VM, VM], out_specs=[VM] *...  7.04 us
    ppermute x12, waiting for transfers between devices, swap_core(): return lax.ppermute(value, 'level', pairs(4, 1))  6.67 us
    unnamed x79, local copies, waits for them, and re-layouts  6.45 us
  transfers between devices with their start and end apart: 27, of which 16 were waited for; matrix products, arithmetic and copies ran while one was open for 6% of the time, Pallas kernels for 43%

profile of v1, /device:TPU:0, one launch (start us, length us, event | category | flops | bytes accessed | tf_op | source)
XLA Modules:
  0.0 193.8 jit_solution(17102872684147080210)
XLA Ops:
  1.8 1.3 reduce_sum.9
  5.6 4.1 %collective-permute-start = (bf16[1,128,256]{2,1,0:T(8,128)(2,1)S(1)}, bf16[1,128,256]{2,1,0:T(8,128)(2,1)S(1)}, u32[]{:S(2)}, u32[]{:S(2)}) collective-permute-start(bf16[1,128,256]{2,1,0:T(8,128)(2,1)S(1)} %fusion.14), channel_id=1, source_target_pairs={{0,16},{4,20},{8,24},{12,28},{16,0},{20,4},{24,8},{28,12},{1,17},{... | collective-permute-start | bytes 196616 | tf_op jit(solution)/shard_map/ppermute | solution.py:1036
  11.2 1.7 pick_rows.1.idx_ref
  13.6 1.3 collective-permute-start.1
  14.8 1.5 collective-permute-start.2
  16.4 2.2 %collective-permute-done.1 = bf16[2,128,256]{2,1,0:T(8,128)(2,1)S(1)} collective-permute-done((bf16[2,128,256]{2,1,0:T(8,128)(2,1)S(1)}, bf16[2,128,256]{2,1,0:T(8,128)(2,1)S(1)}, u32[]{:S(2)}, u32[]{:S(2)}) %collective-permute-start.1) | collective-permute-done | bytes 131104 | tf_op jit(solution)/shard_map/ppermute | solution.py:1040
  18.6 2.1 %collective-permute-done.2 = bf16[1,368,256]{2,1,0:T(8,128)(2,1)S(1)} collective-permute-done((bf16[1,368,256]{2,1,0:T(8,128)(2,1)S(1)}, bf16[1,368,256]{2,1,0:T(8,128)(2,1)S(1)}, u32[]{:S(2)}, u32[]{:S(2)}) %collective-permute-start.2) | collective-permute-done | bytes 188448 | tf_op jit(solution)/shard_map/ppermute | solution.py:1041
  21.5 1.5 collective-permute-start.3
  23.1 5.0 %collective-permute-done.3 = bf16[4,128,256]{2,1,0:T(8,128)(2,1)S(1)} collective-permute-done((bf16[4,128,256]{2,1,0:T(8,128)(2,1)S(1)}, bf16[4,128,256]{2,1,0:T(8,128)(2,1)S(1)}, u32[]{:S(2)}, u32[]{:S(2)}) %collective-permute-start.3) | collective-permute-done | bytes 262176 | tf_op jit(solution)/shard_map/ppermute | solution.py:1045
  30.9 7.0 %front_forward.1 = (bf16[4,256,256]{2,1,0:T(8,128)(2,1)}, bf16[256,384]{1,0:T(8,128)(2,1)}, bf16[256,256]{1,0:T(8,128)(2,1)}, f32[24,256]{1,0:T(8,128)}, f32[1,1...) custom-call(s32[4]{0:T(128)} %pad_add_fusion.1.ids_ref, ...), custom_call_target="tpu_custom_call" | custom-call | flops 1000000000 | bytes 5000000 | tf_op jit(solution)/shard_map/front_forward/pallas_call | solution.py:645
  40.7 3.0 %collective-permute-start.9 = (bf16[4,368,256]{2,1,0:T(8,128)(2,1)S(1)}, bf16[4,368,256]{2,1,0:T(8,128)(2,1)}, u32[]{:S(2)}, u32[]{:S(2)}) collective-permute-start(bf16[4,368,256]{2,1,0:T(8,128)(2,1)S(1)} %constant_dynamic-update-slice_fusion.7.late_a), channel_id=1, source_target_pairs={{0,16},{4,20},{8,24},{12,28},{16,0},{20,4},{24,8},{28,12},{1,17},{... | collective-permute-start | bytes 2261000 | tf_op jit(solution)/shard_map/ppermute | solution.py:1106
  44.4 31.2 %sample_forward.1 = (bf16[8,1216,256]{2,1,0:T(8,128)(2,1)}, bf16[304,256]{1,0:T(8,128)(2,1)}, bf16[304,256]{1,0:T(8,128)(2,1)}) custom-call(s32[4,32,152]{2,1,0:T(8,128)} %pick_rows.1.idx_ref, s32[2,2]{1,0:T(2,128)} %size_ref.5, s32[4]{0:T(128)} %pad_add_fusion.1.ids_ref, bf16[1,16700,2,256]{3,2,1,0:T(2,128)(2,1)} %bitcast.97, ...), custom_call_target="tpu_custom_call" | custom-call | flops 30000001024 | bytes 60000000 | tf_op jit(solution)/shard_map/sample_forward/pallas_call | solution.py:322
  79.4 5.4 %collective-permute-done.8.add_ref = bf16[304,256]{1,0:T(8,128)(2,1)S(1)} collective-permute-done((bf16[304,256]{1,0:T(8,128)(2,1)S(1)}, bf16[304,256]{1,0:T(8,128)(2,1)S(1)}, u32[]{:S(2)}, u32[]{:S(2)}) %collective-permute-start.8) | collective-permute-done | bytes 155680 | tf_op jit(solution)/shard_map/ppermute | solution.py:1000
  84.9 17.4 %post_step.1 = (bf16[304,256]{1,0:T(8,128)(2,1)S(1)}, f32[304,256]{1,0:T(8,128)S(1)}, bf16[8,384,256]{2,1,0:T(8,128)(2,1)S(1)}, bf16[8,384,256]{2,1,0:T(8,128)(2,1)S(1)}, f32[24,256]{1,0:T(8,128)S(1)}) custom-call(s32[4]{0:T(128)S(1)} %copy-done.15, s32[2,32]{1,0:T(2,128)S(1)} %copy-done.21, s32[2]{0:T(128)S(1)} %copy-done.22, ...), custom_call_target="tpu_custom_call" | custom-call | flops 8000000000 | bytes 10000000 | tf_op jit(solution)/shard_map/post_step/pallas_call | solution.py:907
  102.5 1.4 collective-permute-done.12.ds_other
  104.0 2.4 %coef_backward.1 = (bf16[304,128]{1,0:T(8,128)(2,1)S(1)}, bf16[304,128]{1,0:T(8,128)(2,1)S(1)}) custom-call(s32[4]{0:T(128)S(1)} %copy-done.15, bf16[8,1216,256]{2,1,0:T(8,128)(2,1)S(1)} %copy-done.23, bf16[304,256]{1,0:T(8,128)(2,1)S(1)} %get-tuple-element.116.ds_mine, bf16[304,256]{1,0:T(8,128)(2,1)S(1)} %collective-permute-done.12.ds_other, ...), custom_call_target="tpu_custom_call" | custom-call | flops 2000000000 | bytes 10000000 | tf_op jit(solution)/shard_map/coef_backward/pallas_call | solution.py:388
  109.7 1.6 copy-done.29
  111.4 1.6 collective-permute-start.15
  113.0 32.1 %sample_backward.1 = bf16[8,32,256]{2,1,0:T(8,128)(2,1)} custom-call(s32[4,32,152]{2,1,0:T(8,128)} %pick_rows.1.idx_ref, s32[2,2]{1,0:T(2,128)} %size_ref.5, s32[4]{0:T(128)} %pad_add_fusion.1.ids_ref, bf16[1,16700,2,256]{3,2,1,0:T(2,128)(2,1)} %bitcast.98, bf16[304,256]{1,0:T(8,128)(2,1)} %copy-done.19, bf16[304,256]{1,0:T(8,128)(2,1)} %copy-done.20, ...), custom_call_target="tpu_custom_call" | custom-call | flops 30000001024 | bytes 60000000 | tf_op jit(solution)/shard_map/sample_backward/pallas_call | solution.py:487
  145.3 1.3 convert_element_type.121
  146.5 1.6 fusion
  148.2 1.2 copy-done.30
  149.5 9.7 %front_backward.1 = (bf16[8,128,256]{2,1,0:T(8,128)(2,1)}, bf16[8,128,256]{2,1,0:T(8,128)(2,1)}) custom-call(s32[4]{0:T(128)} %pad_add_fusion.1.ids_ref, bf16[2,304,128]{2,1,0:T(8,128)(2,1)} %pad_maximum_fusion.3.near_ref, bf16[2,304,128]{2,1,0:T(8,128)(2,1)} %collective-permute-done.16.far_ref, f32[304,128]{1,0:T(8,128)} %get-tuple-element.105.att_ref, ...), custom_call_target="tpu_custom_call" | custom-call | flops 2000000000 | bytes 5000000 | tf_op jit(solution)/shard_map/front_backward/pallas_call | solution.py:708
  159.2 1.1 add_convert_fusion.1
  160.8 1.1 collective-permute-done.19
  164.7 8.1 %collective-permute-done.21 = bf16[4,128,256]{2,1,0:T(8,128)(2,1)S(1)} collective-permute-done((bf16[4,128,256]{2,1,0:T(8,128)(2,1)S(1)}, bf16[4,128,256]{2,1,0:T(8,128)(2,1)S(1)}, u32[]{:S(2)}, u32[]{:S(2)}) %collective-permute-start.21) | collective-permute-done | bytes 262176 | tf_op jit(solution)/shard_map/ppermute | solution.py:1075
  173.0 2.1 %collective-permute-start.22 = (bf16[2,128,256]{2,1,0:T(8,128)(2,1)S(1)}, bf16[2,128,256]{2,1,0:T(8,128)(2,1)S(1)}, u32[]{:S(2)}, u32[]{:S(2)}) collective-permute-start(bf16[2,128,256]{2,1,0:T(8,128)(2,1)S(1)} %fusion.12), channel_id=1, source_target_pairs={{0,8},{4,12},{8,0},{12,4},{16,24},{20,28},{24,16},{28,20},{1,9},{5... | collective-permute-start | bytes 393224 | tf_op jit(solution)/shard_map/ppermute | solution.py:1075
  175.1 3.9 %collective-permute-done.22 = bf16[2,128,256]{2,1,0:T(8,128)(2,1)S(1)} collective-permute-done((bf16[2,128,256]{2,1,0:T(8,128)(2,1)S(1)}, bf16[2,128,256]{2,1,0:T(8,128)(2,1)S(1)}, u32[]{:S(2)}, u32[]{:S(2)}) %collective-permute-start.22) | collective-permute-done | bytes 131104 | tf_op jit(solution)/shard_map/ppermute | solution.py:1075
  179.1 2.1 %collective-permute-start.23 = (bf16[1,128,256]{2,1,0:T(8,128)(2,1)S(1)}, bf16[1,128,256]{2,1,0:T(8,128)(2,1)S(1)}, u32[]{:S(2)}, u32[]{:S(2)}) collective-permute-start(bf16[1,128,256]{2,1,0:T(8,128)(2,1)S(1)} %fusion.15), channel_id=1, source_target_pairs={{0,16},{4,20},{8,24},{12,28},{16,0},{20,4},{24,8},{28,12},{1,17},{... | collective-permute-start | bytes 196616 | tf_op jit(solution)/shard_map/ppermute | solution.py:1075
  181.2 7.1 %collective-permute-done.25 = bf16[1,384,256]{2,1,0:T(8,128)(2,1)S(1)} collective-permute-done((bf16[1,384,256]{2,1,0:T(8,128)(2,1)S(1)}, bf16[1,384,256]{2,1,0:T(8,128)(2,1)S(1)}, u32[]{:S(2)}, u32[]{:S(2)}) %collective-permute-start.25) | collective-permute-done | bytes 196640 | tf_op jit(solution)/shard_map/ppermute | solution.py:1075
  189.6 1.4 collective-permute-done.24.last_other
  191.2 2.4 %apply_updates.1 = (f32[1,1]{1,0:T(1,128)}, f32[32,384]{1,0:T(8,128)}, bf16[32,384]{1,0:T(8,128)(2,1)}, f32[32,384]{1,0:T(8,128)}, f32[32,384]{1,0:T(8,128)}, /*...) custom-call(s32[4]{0:T(128)S(1)} %copy-done.16, ...), custom_call_target="tpu_custom_call" | custom-call | flops 3000000 | bytes 8000000 | tf_op jit(solution)/shard_map/apply_updates/pallas_call | solution.py:979
  (159 shorter events, 24.3 us)
Async XLA Ops:
  5.6 7.8 %collective-permute-start = (bf16[1,128,256]{2,1,0:T(8,128)(2,1)S(1)}, bf16[1,128,256]{2,1,0:T(8,128)(2,1)S(1)}, u32[]{:S(2)}, u32[]{:S(2)}) collective-permute-start(bf16[1,128,256]{2,1,0:T(8,128)(2,1)S(1)} %fusion.14), channel_id=1, source_target_pairs={{0,16},{4,20},{8,24},{12,28},{16,0},{20,4},{24,8},{28,12},{1,17},{... | collective-permute-start | bytes 196616 | tf_op jit(solution)/shard_map/ppermute | solution.py:1036
  13.6 5.0 %collective-permute-start.1 = (bf16[2,128,256]{2,1,0:T(8,128)(2,1)S(1)}, bf16[2,128,256]{2,1,0:T(8,128)(2,1)S(1)}, u32[]{:S(2)}, u32[]{:S(2)}) collective-permute-start(bf16[2,128,256]{2,1,0:T(8,128)(2,1)S(1)} %pad_maximum_fusion.4), channel_id=1, source_target_pairs={{0,8},{4,12},{8,0},{12,4},{16,24},{20,28},{24,16},{28,20},{1,9},{5... | collective-permute-start | bytes 393224 | tf_op jit(solution)/shard_map/ppermute | solution.py:1040
  14.8 5.9 %collective-permute-start.2 = (bf16[1,368,256]{2,1,0:T(8,128)(2,1)S(1)}, bf16[1,368,256]{2,1,0:T(8,128)(2,1)S(1)}, u32[]{:S(2)}, u32[]{:S(2)}) collective-permute-start(bf16[1,368,256]{2,1,0:T(8,128)(2,1)S(1)} %constant_dynamic-slice_fusion), channel_id=1, source_target_pairs={{0,4},{4,0},{8,12},{12,8},{16,20},{20,16},{24,28},{28,24},{1,5},{5... | collective-permute-start | bytes 565256 | tf_op jit(solution)/shard_map/ppermute | solution.py:1041
  21.5 6.6 %collective-permute-start.3 = (bf16[4,128,256]{2,1,0:T(8,128)(2,1)S(1)}, bf16[4,128,256]{2,1,0:T(8,128)(2,1)S(1)}, u32[]{:S(2)}, u32[]{:S(2)}) collective-permute-start(bf16[4,128,256]{2,1,0:T(8,128)(2,1)S(1)} %pad_maximum_fusion.2), channel_id=1, source_target_pairs={{0,4},{4,0},{8,12},{12,8},{16,20},{20,16},{24,28},{28,24},{1,5},{5... | collective-permute-start | bytes 786440 | tf_op jit(solution)/shard_map/ppermute | solution.py:1045
  28.1 2.0 %collective-permute-start.4 = (bf16[8,128,256]{2,1,0:T(8,128)(2,1)S(1)}, bf16[8,128,256]{2,1,0:T(8,128)(2,1)S(1)}, u32[]{:S(2)}, u32[]{:S(2)}) collective-permute-start(bf16[8,128,256]{2,1,0:T(8,128)(2,1)S(1)} %constant_dynamic-update-slice_fusion.5.mine_ref), channel_id=1, source_target_pairs={{0,1},{1,0},{2,3},{3,2},{4,5},{5,4},{6,7},{7,6},{8,9},{9,8},{10,11... | collective-permute-start | bytes 1572872 | tf_op jit(solution)/shard_map/ppermute | solution.py:996
  28.2 11.5 %collective-permute-start.5 = (bf16[2,368,256]{2,1,0:T(8,128)(2,1)}, bf16[2,368,256]{2,1,0:T(8,128)(2,1)}, u32[]{:S(2)}, u32[]{:S(2)}) collective-permute-start(bf16[2,368,256]{2,1,0:T(8,128)(2,1)} %pad_maximum_fusion.1), channel_id=1, source_target_pairs={{0,8},{4,12},{8,0},{12,4},{16,24},{20,28},{24,16},{28,20},{1,9},{5... | collective-permute-start | bytes 1130504 | tf_op jit(solution)/shard_map/ppermute | solution.py:1046
  38.0 5.8 %collective-permute-start.6 = (f32[304,128]{1,0:T(8,128)}, f32[304,128]{1,0:T(8,128)S(1)}, u32[]{:S(2)}, u32[]{:S(2)}) collective-permute-start(f32[304,128]{1,0:T(8,128)} %get-tuple-element.109), channel_id=1, source_target_pairs={{0,1},{1,0},{2,3},{3,2},{4,5},{5,4},{6,7},{7,6},{8,9},{9,8},{10,11... | collective-permute-start | bytes 466952 | tf_op jit(solution)/shard_map/ppermute | solution.py:996
  40.7 36.6 %collective-permute-start.9 = (bf16[4,368,256]{2,1,0:T(8,128)(2,1)S(1)}, bf16[4,368,256]{2,1,0:T(8,128)(2,1)}, u32[]{:S(2)}, u32[]{:S(2)}) collective-permute-start(bf16[4,368,256]{2,1,0:T(8,128)(2,1)S(1)} %constant_dynamic-update-slice_fusion.7.late_a), channel_id=1, source_target_pairs={{0,16},{4,20},{8,24},{12,28},{16,0},{20,4},{24,8},{28,12},{1,17},{... | collective-permute-start | bytes 2261000 | tf_op jit(solution)/shard_map/ppermute | solution.py:1106
  44.4 40.4 %copy-start.15 = (s32[4]{0:T(128)S(1)}, s32[4]{0:T(128)}, u32[]{:S(2)}) copy-start(s32[4]{0:T(128)} %pad_add_fusion.1.ids_ref) | copy-start | bytes 52
  44.4 40.4 %copy-start.21 = (s32[2,32]{1,0:T(2,128)S(1)}, s32[2,32]{1,0:T(2,128)}, u32[]{:S(2)}) copy-start(s32[2,32]{1,0:T(2,128)} %match_ref.1) | copy-start | bytes 772
  44.4 40.4 %copy-start.22 = (s32[2]{0:T(128)S(1)}, s32[2]{0:T(128)}, u32[]{:S(2)}) copy-start(s32[2]{0:T(128)} %count_ref.1) | copy-start | bytes 28
  44.4 40.4 %copy-start.24 = (f32[304,256]{1,0:T(8,128)S(1)}, f32[304,256]{1,0:T(8,128)}, u32[]{:S(2)}) copy-start(f32[304,256]{1,0:T(8,128)} %get-tuple-element.113.dec_ref) | copy-start | bytes 933892
  44.4 40.4 %copy-start.27 = (f32[24,256]{1,0:T(8,128)S(1)}, f32[24,256]{1,0:T(8,128)}, u32[]{:S(2)}) copy-start(f32[24,256]{1,0:T(8,128)} %get-tuple-element.115.vec_ref) | copy-start | bytes 73732
  75.7 1.7 collective-permute-start.7
  75.8 9.1 %collective-permute-start.10 = (bf16[4,368,256]{2,1,0:T(8,128)(2,1)S(1)}, bf16[4,368,256]{2,1,0:T(8,128)(2,1)S(1)}, u32[]{:S(2)}, u32[]{:S(2)}) collective-permute-start(bf16[4,368,256]{2,1,0:T(8,128)(2,1)S(1)} %constant_dynamic-update-slice_fusion.7.late_a), channel_id=1, source_target_pairs={{0,1},{1,0},{2,3},{3,2},{4,5},{5,4},{6,7},{7,6},{8,9},{9,8},{10,11... | collective-permute-start | bytes 2261000 | tf_op jit(solution)/shard_map/ppermute | solution.py:996
  77.4 7.5 %collective-permute-start.11 = (bf16[4,368,256]{2,1,0:T(8,128)(2,1)}, bf16[4,368,256]{2,1,0:T(8,128)(2,1)}, u32[]{:S(2)}, u32[]{:S(2)}) collective-permute-start(bf16[4,368,256]{2,1,0:T(8,128)(2,1)} %collective-permute-done.9.late_b), channel_id=1, source_target_pairs={{0,1},{1,0},{2,3},{3,2},{4,5},{5,4},{6,7},{7,6},{8,9},{9,8},{10,11... | collective-permute-start | bytes 2261000 | tf_op jit(solution)/shard_map/ppermute | solution.py:996
  78.5 6.4 %collective-permute-start.8 = (bf16[304,256]{1,0:T(8,128)(2,1)S(1)}, bf16[304,256]{1,0:T(8,128)(2,1)S(1)}, u32[]{:S(2)}, u32[]{:S(2)}) collective-permute-start(bf16[304,256]{1,0:T(8,128)(2,1)S(1)} %add_convert_fusion.s_ref), channel_id=1, source_target_pairs={{0,2},{1,3},{2,0},{3,1},{4,6},{5,7},{6,4},{7,5},{8,10},{9,11},{10,... | collective-permute-start | bytes 466952 | tf_op jit(solution)/shard_map/ppermute | solution.py:1000
  102.4 1.4 collective-permute-start.12
  103.8 5.5 %collective-permute-start.14 = (bf16[8,384,256]{2,1,0:T(8,128)(2,1)S(1)}, bf16[8,384,256]{2,1,0:T(8,128)(2,1)S(1)}, u32[]{:S(2)}, u32[]{:S(2)}) collective-permute-start(bf16[8,384,256]{2,1,0:T(8,128)(2,1)S(1)} %get-tuple-element.121), channel_id=1, source_target_pairs={{0,1},{1,0},{2,3},{3,2},{4,5},{5,4},{6,7},{7,6},{8,9},{9,8},{10,11... | collective-permute-start | bytes 4718600 | tf_op jit(solution)/shard_map/ppermute | solution.py:996
  106.4 1.3 collective-permute-start.13
  108.4 41.0 %collective-permute-start.16 = (bf16[2,304,128]{2,1,0:T(8,128)(2,1)}, bf16[2,304,128]{2,1,0:T(8,128)(2,1)}, u32[]{:S(2)}, u32[]{:S(2)}) collective-permute-start(bf16[2,304,128]{2,1,0:T(8,128)(2,1)} %pad_maximum_fusion.3.near_ref), channel_id=1, source_target_pairs={{0,2},{1,3},{2,0},{3,1},{4,6},{5,7},{6,4},{7,5},{8,10},{9,11},{10,... | collective-permute-start | bytes 466952 | tf_op jit(solution)/shard_map/ppermute | solution.py:1000
  111.4 33.8 %collective-permute-start.15 = (bf16[4,384,256]{2,1,0:T(8,128)(2,1)S(1)}, bf16[4,384,256]{2,1,0:T(8,128)(2,1)}, u32[]{:S(2)}, u32[]{:S(2)}) collective-permute-start(bf16[4,384,256]{2,1,0:T(8,128)(2,1)S(1)} %fusion.1), channel_id=1, source_target_pairs={{0,4},{4,0},{8,12},{12,8},{16,20},{20,16},{24,28},{28,24},{1,5},{5... | collective-permute-start | bytes 2359304 | tf_op jit(solution)/shard_map/ppermute | solution.py:1075
  145.2 14.1 %collective-permute-start.18 = (bf16[8,32,256]{2,1,0:T(8,128)(2,1)}, bf16[8,32,256]{2,1,0:T(8,128)(2,1)}, u32[]{:S(2)}, u32[]{:S(2)}) collective-permute-start(bf16[8,32,256]{2,1,0:T(8,128)(2,1)} %sample_backward.1), channel_id=1, source_target_pairs={{0,2},{1,3},{2,0},{3,1},{4,6},{5,7},{6,4},{7,5},{8,10},{9,11},{10,... | collective-permute-start | bytes 393224 | tf_op jit(solution)/shard_map/ppermute | solution.py:1000
  149.4 13.5 %collective-permute-start.20 = (bf16[2,384,256]{2,1,0:T(8,128)(2,1)S(1)}, bf16[2,384,256]{2,1,0:T(8,128)(2,1)S(1)}, u32[]{:S(2)}, u32[]{:S(2)}) collective-permute-start(bf16[2,384,256]{2,1,0:T(8,128)(2,1)S(1)} %fusion.5), channel_id=1, source_target_pairs={{0,8},{4,12},{8,0},{12,4},{16,24},{20,28},{24,16},{28,20},{1,9},{5... | collective-permute-start | bytes 1179656 | tf_op jit(solution)/shard_map/ppermute | solution.py:1075
  159.2 3.8 %collective-permute-start.17 = (bf16[8,128,256]{2,1,0:T(8,128)(2,1)}, bf16[8,128,256]{2,1,0:T(8,128)(2,1)S(1)}, u32[]{:S(2)}, u32[]{:S(2)}) collective-permute-start(bf16[8,128,256]{2,1,0:T(8,128)(2,1)} %get-tuple-element.138), channel_id=1, source_target_pairs={{0,1},{1,0},{2,3},{3,2},{4,5},{5,4},{6,7},{7,6},{8,9},{9,8},{10,11... | collective-permute-start | bytes 1572872 | tf_op jit(solution)/shard_map/ppermute | solution.py:996
  160.4 1.6 collective-permute-start.19
  164.1 8.6 %collective-permute-start.21 = (bf16[4,128,256]{2,1,0:T(8,128)(2,1)S(1)}, bf16[4,128,256]{2,1,0:T(8,128)(2,1)S(1)}, u32[]{:S(2)}, u32[]{:S(2)}) collective-permute-start(bf16[4,128,256]{2,1,0:T(8,128)(2,1)S(1)} %fusion.8), channel_id=1, source_target_pairs={{0,4},{4,0},{8,12},{12,8},{16,20},{20,16},{24,28},{28,24},{1,5},{5... | collective-permute-start | bytes 786440 | tf_op jit(solution)/shard_map/ppermute | solution.py:1075
  173.0 6.0 %collective-permute-start.22 = (bf16[2,128,256]{2,1,0:T(8,128)(2,1)S(1)}, bf16[2,128,256]{2,1,0:T(8,128)(2,1)S(1)}, u32[]{:S(2)}, u32[]{:S(2)}) collective-permute-start(bf16[2,128,256]{2,1,0:T(8,128)(2,1)S(1)} %fusion.12), channel_id=1, source_target_pairs={{0,8},{4,12},{8,0},{12,4},{16,24},{20,28},{24,16},{28,20},{1,9},{5... | collective-permute-start | bytes 393224 | tf_op jit(solution)/shard_map/ppermute | solution.py:1075
  175.1 13.2 %collective-permute-start.25 = (bf16[1,384,256]{2,1,0:T(8,128)(2,1)S(1)}, bf16[1,384,256]{2,1,0:T(8,128)(2,1)S(1)}, u32[]{:S(2)}, u32[]{:S(2)}) collective-permute-start(bf16[1,384,256]{2,1,0:T(8,128)(2,1)S(1)} %fusion.11), channel_id=1, source_target_pairs={{0,16},{4,20},{8,24},{12,28},{16,0},{20,4},{24,8},{28,12},{1,17},{... | collective-permute-start | bytes 589832 | tf_op jit(solution)/shard_map/ppermute | solution.py:1075
  179.1 9.9 %collective-permute-start.23 = (bf16[1,128,256]{2,1,0:T(8,128)(2,1)S(1)}, bf16[1,128,256]{2,1,0:T(8,128)(2,1)S(1)}, u32[]{:S(2)}, u32[]{:S(2)}) collective-permute-start(bf16[1,128,256]{2,1,0:T(8,128)(2,1)S(1)} %fusion.15), channel_id=1, source_target_pairs={{0,16},{4,20},{8,24},{12,28},{16,0},{20,4},{24,8},{28,12},{1,17},{... | collective-permute-start | bytes 196616 | tf_op jit(solution)/shard_map/ppermute | solution.py:1075
  189.1 2.0 %collective-permute-start.26 = (f32[384,256]{1,0:T(8,128)S(1)}, f32[384,256]{1,0:T(8,128)S(1)}, u32[]{:S(2)}, u32[]{:S(2)}) collective-permute-start(f32[384,256]{1,0:T(8,128)S(1)} %fusion.7.late_mine), channel_id=1, source_target_pairs={{0,1},{1,0},{2,3},{3,2},{4,5},{5,4},{6,7},{7,6},{8,9},{9,8},{10,11... | collective-permute-start | bytes 1179656 | tf_op jit(solution)/shard_map/ppermute | solution.py:996
  189.1 1.9 collective-permute-start.24
  (32 other events, 412.8 us)

commit v2 on v1

--- a/solution.py
+++ b/solution.py
@@ -23,6 +23,12 @@
 RS = D // SHARDS
 EARLY_BITS = (4, 2, 1)
 LATE_BITS = (1, 2, 4)
+EARLY_SUM_BITS = (1, 2, 4)
+LATE_SUM_BITS = (1, 2, 4)
+
+
+def place(shard, bits):
+    return sum((shard >> (bit // 2) & 1) << 2 - i for i, bit in enumerate(bits))
 BF = jnp.bfloat16
 F32 = jnp.float32
 VMEM_LIMIT = 62 * 1024 * 1024
@@ -98,7 +104,7 @@
 class Chunks:
     def __init__(self, mem_ref, buf, stage, sems, size_ref, ids_ref):
         self.mem_ref, self.buf, self.stage, self.sems = mem_ref, buf, stage, sems
-        self.cells = buf.shape[1]
+        self.slots, self.cells = buf.shape[:2]
         level = ids_ref[0]
         self.high, self.wide = (
             [(size_ref[f, axis] + (1 << level) - 1) >> level for f in range(2)] for axis in range(2)
@@ -126,21 +132,23 @@
             for c in range(COPIES)
         ]
 
-    def start(self, j, slot):
-        for copy in self.copies(j, slot):
-            copy.start()
+    def start(self, j):
+        @pl.when(j < self.count)
+        def _():
+            for copy in self.copies(j, lax.rem(j, self.slots)):
+                copy.start()
+
+    def start_all(self):
+        for j in range(self.slots - 1):
+            self.start(jnp.int32(j))
 
     def staged(self, i, f, j):
         return pl.ds(2 * (i * self.wide[f] - self.base(j) + STRIDE) + f, STRIDE, 2)
 
     def run(self, work):
         def body(j, carry):
-            slot = j % 2
-
-            @pl.when(j + 1 < self.count)
-            def _():
-                self.start(j + 1, 1 - slot)
-
+            slot = lax.rem(j, self.slots)
+            self.start(j + self.slots - 1)
             for copy in self.copies(j, slot):
                 copy.wait()
             work(j, self.buf[slot].reshape(2 * self.cells, D))
@@ -195,7 +203,7 @@
 ):
     own = ids_ref[1]
     chunks = Chunks(mem_ref, buf, stage, sems, size_ref, ids_ref)
-    chunks.start(0, 0)
+    chunks.start_all()
     for copy in pick_copies(idx_ref, picks, isem):
         copy.start()
     place_coefs(join_frames(own, mine_ref, other_ref, fscr), cscr)
@@ -289,9 +297,9 @@
 VM = pl.BlockSpec(memory_space=pltpu.VMEM)
 
 
-def sampling_scratch(cells):
+def sampling_scratch(slots, cells):
     return [
-        pltpu.VMEM((2, cells, 2, D), BF),
+        pltpu.VMEM((slots, cells, 2, D), BF),
         pltpu.VMEM((2, 2 * (cells + 2 * STRIDE), 128), F32),
         [[pltpu.VMEM((TABLE, 128), F32)] * 2] * 2,
         pltpu.VMEM((8, 2 * R, D), BF),
@@ -301,8 +309,8 @@
     ]
 
 
-def sampling_semaphores():
-    return [pltpu.SemaphoreType.DMA((2, COPIES)), pltpu.SemaphoreType.DMA(())]
+def sampling_semaphores(slots):
+    return [pltpu.SemaphoreType.DMA((slots, COPIES)), pltpu.SemaphoreType.DMA(())]
 
 
 def pick_scratch():
@@ -324,9 +332,9 @@
         in_specs=[ANY, SM, SM, ANY, VM, VM, VM],
         out_specs=[ANY, VM, VM],
         out_shape=[jax.ShapeDtypeStruct((8, 2 * R, D), BF), frame, frame],
-        scratch_shapes=sampling_scratch(1680)
+        scratch_shapes=sampling_scratch(4, 1680)
         + [pltpu.VMEM((8, 2 * R, D), BF), pltpu.VMEM((16, 16, 128), F32)]
-        + sampling_semaphores()
+        + sampling_semaphores(4)
         + [pltpu.SemaphoreType.DMA((NB // 2 // STAGE,))]
         + pick_scratch(),
         compiler_params=params(),
@@ -411,7 +419,7 @@
     chunks = Chunks(mem_ref, buf, stage, sems, size_ref, ids_ref)
     for copy in pick_copies(idx_ref, picks, isem):
         copy.start()
-    chunks.start(0, 0)
+    chunks.start_all()
     place_coefs(join_frames(own, fa_mine, fa_other, fscr), cscr)
     fill_weights(cscr, wexp)
     place_grads(join_frames(own, ds_mine, ds_other, dscr), g2)
@@ -480,7 +488,7 @@
 
     chunks.run(reduce)
     for n in range(SHARDS):
-        out_ref[ids_ref[2] ^ n] = sum_ref[n * RS : (n + 1) * RS].astype(BF)
+        out_ref[place(ids_ref[2] ^ n, EARLY_SUM_BITS)] = sum_ref[n * RS : (n + 1) * RS].astype(BF)
 
 
 def sample_backward(idx, size, ids, memory_t, ds_mine, ds_other, fa_mine, fa_other):
@@ -489,7 +497,7 @@
         in_specs=[ANY, SM, SM, ANY] + [VM] * 4,
         out_specs=VM,
         out_shape=jax.ShapeDtypeStruct((SHARDS, RS, D), BF),
-        scratch_shapes=sampling_scratch(3344) + [pltpu.VMEM((2, FR, D), BF)] + sampling_semaphores() + [pltpu.VMEM((D, D), F32)] + pick_scratch(),
+        scratch_shapes=sampling_scratch(2, 3344) + [pltpu.VMEM((2, FR, D), BF)] + sampling_semaphores(2) + [pltpu.VMEM((D, D), F32)] + pick_scratch(),
         compiler_params=params(),
         cost_estimate=cost(30_000_000_000, 60_000_000),
         name="sample_backward",
@@ -574,6 +582,57 @@
     return x
 
 
+LATE = 23 * RS // 2
+
+
+def early_kernel(ids_ref, count_ref, square_ref, query_ref, vec_ref, out_ref):
+    own, me = ids_ref[1], ids_ref[2]
+    count = sum(count_ref[i] for i in range(count_ref.shape[0])).astype(F32)
+    row, lane = lax.broadcasted_iota(jnp.int32, (24, RS), 0), jnp.zeros((24, 128 - RS), F32)
+    vec = jnp.concatenate([vec_ref[...], jnp.zeros((3, RS), F32)], 0)
+    vec = jnp.concatenate([jnp.where(row == 21, count, vec), lane], 1)
+    vec = pltpu.roll(vec, me % 4 * RS, 1)
+    zero = jnp.zeros_like(vec)
+    vec = jnp.concatenate([jnp.where(me < 4, vec, zero), jnp.where(me < 4, zero, vec)], 1)
+    first = square_ref[:4].reshape(4 * RS, D)
+    right = jnp.concatenate([query_ref[: RS // 2, D:], query_ref[RS // 2 :, D:]], 1)
+    second = jnp.concatenate([square_ref[4], query_ref[:, :D], right, vec, jnp.zeros((24, D), F32)], 0)
+    out_ref[0] = jnp.where(own == 0, first, second).astype(BF)
+
+
+def pack_early(ids, count, square, query, vec):
+    return pl.pallas_call(
+        early_kernel,
+        grid=(1,),
+        in_specs=[SM, SM, pl.BlockSpec((5, RS, D), lambda i: (0, 0, 0)), VM, VM],
+        out_specs=VM,
+        out_shape=jax.ShapeDtypeStruct((1, 128, D), BF),
+        name="pack_early",
+    )(ids, count, square, query, vec)
+
+
+def late_kernel(ids_ref, square_ref, in_ref, out_weight_ref, out_ref, all_ref):
+    for m in range(7):
+        all_ref[m * RS : (m + 1) * RS] = square_ref[5 + m].astype(BF)
+    for i in range(2):
+        for c in range(4):
+            row = (7 + 4 * i + c) * RS
+            all_ref[row : row + RS] = in_ref[i, :, c * D : (c + 1) * D].astype(BF)
+        all_ref[(15 + 4 * i) * RS : (19 + 4 * i) * RS] = out_weight_ref[i].astype(BF)
+    out_ref[0] = all_ref[pl.ds(pl.multiple_of(ids_ref[1] * LATE, 16), LATE)]
+
+
+def pack_late(ids, square, ffn_in, ffn_out):
+    return pl.pallas_call(
+        late_kernel,
+        in_specs=[SM, VM, VM, VM],
+        out_specs=VM,
+        out_shape=jax.ShapeDtypeStruct((1, LATE, D), BF),
+        scratch_shapes=[pltpu.VMEM((2 * LATE, D), BF)],
+        name="pack_late",
+    )(ids, square, ffn_in, ffn_out)
+
+
 def order(bits):
     return [sum(bit for i, bit in enumerate(bits) if n >> i & 1) for n in range(SHARDS)]
 
@@ -603,12 +662,14 @@
 
 def front_kernel(
     ids_ref, x_ref, mine_ref, other_ref,
-    w_ref, wq_ref, s4_ref, vec_ref, total_ref, dec_ref, y_ref, q_ref, k_ref, v_ref, m_ref, p_ref, fa_ref, send_ref, att_ref,
+    w_ref, wq_ref, s4_ref, vec_ref, total_ref, xb_ref, dec_ref, y_ref, q_ref, k_ref, v_ref, m_ref, p_ref, fa_ref, send_ref, att_ref,
 ):
     unpack_early(ids_ref[2], ids_ref[1], mine_ref, other_ref, w_ref, wq_ref, s4_ref, vec_ref)
     total_ref[...] = jnp.sum(vec_ref[21:22], -1, keepdims=True) / RS
-    x = jnp.concatenate([x_ref[...].astype(F32), jnp.zeros((FR - Q, D), F32)], 0)
-    y, _, q, k, v, mixed = attend_forward(x, w_ref[0], w_ref[1], w_ref[2], w_ref[3], vec_ref[10:11], p_ref)
+    x = x_ref[...].astype(F32)
+    x = jnp.where(ids_ref[1] == 0, x[:Q], x[Q:])
+    x = jnp.concatenate([x, jnp.zeros((FR - Q, D), F32)], 0)
+    y, xb_ref[...], q, k, v, mixed = attend_forward(x, w_ref[0], w_ref[1], w_ref[2], w_ref[3], vec_ref[10:11], p_ref)
     y_ref[...], q_ref[...], k_ref[...], v_ref[...], m_ref[...] = y, q, k, v, mixed
     dec, _, _ = norm_forward(y, vec_ref[0:1], vec_ref[1:2])
     dec_ref[...] = dec
@@ -645,8 +706,9 @@
     return pl.pallas_call(
         front_kernel,
         in_specs=[SM, VM, VM, VM],
-        out_specs=[VM] * 15,
+        out_specs=[VM] * 16,
         out_shape=WEIGHT_SHAPES
+        + [frame_rows(BF)]
         + [frame_rows(F32)] * 2
         + [frame_rows(BF)] * 4
         + [jax.ShapeDtypeStruct((H, FR, FR), BF)]
@@ -678,7 +740,7 @@
     d_dec = dres_ref[...] + dot_nt(grad, wq_ref[...])
     _, unit, rstd = norm_forward(y_ref[...], vec_ref[0:1], vec_ref[1:2])
     dy, d_gain, d_shift = norm_backward(d_dec, unit, rstd, vec_ref[0:1])
-    xb = jnp.concatenate([x_ref[...].astype(F32), jnp.zeros((FR - Q, D), F32)], 0).astype(BF)
+    xb = x_ref[...]
     _, d_w = attend_backward(
         dy, xb, q_ref[...], k_ref[...], v_ref[...], m_ref[...], p_ref, w_ref[0], w_ref[1], w_ref[2], w_ref[3]
     )
@@ -690,7 +752,7 @@
     d_vec = d_vec.astype(BF)
     first, second = own, 1 - own
     for shard in range(SHARDS):
-        n = me ^ shard
+        n = place(me ^ shard, EARLY_SUM_BITS)
         at = slice(shard * RS, (shard + 1) * RS)
         for m in range(4):
             all_ref[first, n, m * RS : (m + 1) * RS] = d_w[m][at]
@@ -740,9 +802,6 @@
 
 
 LOSS_UNITS = [16.0 ** (3 - n) for n in range(8)]
-LATE = 23 * RS // 2
-
-
 def unpack_late(me, own, mine, other, ws_ref, fi_ref, fo_ref):
     def take(halves):
         for n in range(SHARDS):
@@ -787,7 +846,7 @@
     def put_square(m, grad):
         grad = grad.astype(BF)
         for n in range(SHARDS):
-            all_ref[kept, me ^ n, m * RS : (m + 1) * RS] = grad[n * RS : (n + 1) * RS]
+            all_ref[kept, place(me ^ n, LATE_SUM_BITS), m * RS : (m + 1) * RS] = grad[n * RS : (n + 1) * RS]
 
     def put_in(i, grad):
         grad = grad.astype(BF)
@@ -795,14 +854,14 @@
             for c in range(4):
                 piece = grad[n * RS : (n + 1) * RS, c * D : (c + 1) * D]
                 if i == 0:
-                    all_ref[kept, me ^ n, (7 + c) * RS : (8 + c) * RS] = piece
+                    all_ref[kept, place(me ^ n, LATE_SUM_BITS), (7 + c) * RS : (8 + c) * RS] = piece
                 else:
-                    all_ref[given, me ^ n, c * RS : (c + 1) * RS] = piece
+                    all_ref[given, place(me ^ n, LATE_SUM_BITS), c * RS : (c + 1) * RS] = piece
 
     def put_out(i, grad):
         grad = grad.astype(BF)
         for n in range(SHARDS):
-            all_ref[given, me ^ n, (4 + 4 * i) * RS : (8 + 4 * i) * RS] = grad[n * 4 * RS : (n + 1) * 4 * RS]
+            all_ref[given, place(me ^ n, LATE_SUM_BITS), (4 + 4 * i) * RS : (8 + 4 * i) * RS] = grad[n * 4 * RS : (n + 1) * 4 * RS]
 
     vec = lambda row: vec_ref[row : row + 1]
     total = lambda value: jnp.sum(value, 0, keepdims=True)
@@ -897,7 +956,7 @@
         above = whole
     rows = rows.astype(BF)
     for n in range(SHARDS):
-        all_ref[kept, me ^ n, 11 * RS : 12 * RS] = rows
+        all_ref[kept, place(me ^ n, LATE_SUM_BITS), 11 * RS : 12 * RS] = rows
     mine_ref[...] = all_ref[0]
     send_ref[...] = all_ref[1]
 
@@ -1008,6 +1067,10 @@
     return jnp.where(index == 0, mine, other), jnp.where(index == 0, other, mine)
 
 
+def after(value, event):
+    return lax.optimization_barrier((value, event))[0]
+
+
 def early_rows(square, query, vec):
     right = jnp.concatenate([query[: RS // 2, D:], query[RS // 2 :, D:]], 1)
     second = jnp.concatenate([square[4], query[:, :D], right, vec, jnp.zeros((24, D), vec.dtype)], 0)
@@ -1025,27 +1088,26 @@
     )
 
 
-def gather_weights(dp, own, rows, w_query, w_square, w_ffn_in, w_ffn_out, vectors, count):
-    rs = D // dp
-    shard = lax.axis_index("dp")
-    here = jnp.arange(D, dtype=jnp.int32)[None, :] // rs == shard
-    vec = jnp.where(here, jnp.tile(jnp.pad(vectors, ((0, 3), (0, 0))), (1, dp)), 0.0)
-    vec = jnp.where(here & (jnp.arange(24)[:, None] == 21), count, vec)
+def gather_weights(dp, ids, own, rows, w_query, w_square, w_ffn_in, w_ffn_out, vectors, counts):
     if dp == SHARDS:
-        early = pick(early_rows(w_square[:5], w_query, vec).astype(BF), own)[None]
+        early = pack_early(ids, counts, w_square, w_query, vectors)
+        early, *late = lax.optimization_barrier((early, w_square, w_ffn_in, w_ffn_out))
         first = lax.ppermute(early, "dp", pairs(dp, EARLY_BITS[0]))
-        early, first, *late = lax.optimization_barrier((early, first, w_square[5:], w_ffn_in, w_ffn_out))
-        late = pick(late_rows(*(w.astype(BF) for w in late)).reshape(2, -1, D), own)[None]
+        late = pack_late(ids, *late)
         early, late, rows = lax.optimization_barrier((jnp.concatenate([early, first], 0), late, rows))
         second = lax.ppermute(early, "dp", pairs(dp, EARLY_BITS[1]))
         late_first = lax.ppermute(late, "dp", pairs(dp, LATE_BITS[0]))
-        early = jnp.concatenate([early, second], 0)
-        late = jnp.concatenate([late, late_first], 0)
-        early, late = lax.optimization_barrier((early, late))
+        early, late_first = lax.optimization_barrier((jnp.concatenate([early, second], 0), late_first))
         third = lax.ppermute(early, "dp", pairs(dp, EARLY_BITS[2]))
+        late = jnp.concatenate([late, after(late_first, third)], 0)
         late = (late, lax.ppermute(late, "dp", pairs(dp, LATE_BITS[1])))
         early = jnp.concatenate([early, third], 0)
         return rows, early, swap_core(early), late
+
+    rs = D // dp
+    here = jnp.arange(D, dtype=jnp.int32)[None, :] // rs == lax.axis_index("dp")
+    vec = jnp.where(here, jnp.tile(jnp.pad(vectors, ((0, 3), (0, 0))), (1, dp)), 0.0)
+    vec = jnp.where(here & (jnp.arange(24)[:, None] == 21), jnp.sum(counts).astype(F32), vec)
 
     def whole(weight, dim):
         return lax.all_gather(weight.astype(BF), "dp", axis=dim, tiled=True)
@@ -1067,16 +1129,12 @@
 
 
 def halve(value):
-    value = value.reshape(-1, 2, *value.shape[1:])
-    return value[:, 0], value[:, 1].astype(BF)
+    count = value.shape[0] // 2
+    return value[:count], value[count:].astype(BF)
 
 
 def send(value, bit):
-    return lax.ppermute(value, "dp", pairs(SHARDS, bit)).astype(F32)
-
-
-def after(value, event):
-    return lax.optimization_barrier((value, event))[0]
+    return lax.ppermute(value, "dp", pairs(SHARDS, bit))
 
 
 def shards(
@@ -1094,11 +1152,10 @@
     ids = jnp.stack([level, own, me, 0]).astype(jnp.int32)
     rows = pick_rows(frame_size, ids, sample_pick[:, 0, :].T)
     rows, mine, other, late = gather_weights(
-        dp, own, rows, w_query, w_square, w_ffn_in, w_ffn_out, vectors, jnp.sum(obj_count).astype(F32)
+        dp, ids, own, rows, w_query, w_square, w_ffn_in, w_ffn_out, vectors, obj_count
     )
     memory_t = memory.transpose(1, 2, 0, 3)
-    x = pick(queries.reshape(2, Q, D), own)
-    w4, wq, s4, vec, total, dec, y, q, k, v, mixed, p, fa, fa_send, att = front_forward(ids, x, mine, other)
+    w4, wq, s4, vec, total, x, dec, y, q, k, v, mixed, p, fa, fa_send, att = front_forward(ids, queries, mine, other)
     fa_other = swap_core(fa_send)
     if dp == SHARDS:
         late = jnp.concatenate([late[0], after(late[1], att)], 0)
@@ -1108,7 +1165,7 @@
     part_other = swap_core(part_send)
     half = (part.astype(F32) + part_other.astype(F32)).astype(BF)
     half_other = swap_chip(half)
-    late_end = after(late[1], part_other)
+    late_end = after(late[1], half)
     late = (late[0], late_end, swap_core(late[0]), swap_core(late_end))
     ds, dres, late_mine, late_send, dvec = post_step(
         ids, match, obj_count, half, half_other, dec, target_box, late, vec
@@ -1118,33 +1175,38 @@
     gp, gp_send = coef_backward(ids, gathered, ds, ds_other, fa, fa_other)
     near = jnp.stack([gp, swap_core(gp_send)])
     far = swap_chip(near)
-    late_sum = late_mine.astype(F32) + late_sent.astype(F32)
-    late_kept, late_out = halve(late_sum)
-    near, late_out, ds_other = lax.optimization_barrier((near, late_out, ds_other))
     if dp == SHARDS:
-        late_in = send(late_out, 1)
+        (keep, out), (keep_other, out_other) = halve(late_mine), halve(late_sent)
+        late_kept = keep.astype(F32) + keep_other.astype(F32)
+        late_out = (out.astype(F32) + out_other.astype(F32)).astype(BF)
+        near, late_out, ds_other = lax.optimization_barrier((near, late_out, ds_other))
+        late_in = send(late_out, LATE_SUM_BITS[0])
+    else:
+        late_sum = late_mine.astype(F32) + late_sent.astype(F32)
     d_s4 = sample_backward(rows, frame_size, ids, memory_t, ds, ds_other, fa, fa_other)
+    if dp == SHARDS:
+        far, late_in, d_s4 = lax.optimization_barrier((far, late_in, d_s4))
+        late_kept, late_out = halve(late_kept + late_in.astype(F32))
+        near, late_out = lax.optimization_barrier((near, late_out))
+        late_in = send(late_out, LATE_SUM_BITS[1])
     d_s4_other = swap_chip(d_s4)
-    if dp == SHARDS:
-        late_kept, late_out = halve(late_kept + after(late_in, d_s4))
-        near, late_out = lax.optimization_barrier((near, late_out))
-        late_in = send(late_out, 2)
     last_mine, last_send = front_backward(
         ids, near, far, att, dres, x, dec, y, q, k, v, mixed, p, w4, wq, vec, dvec
     )
-    d_s4 = (d_s4.astype(F32) + d_s4_other.astype(F32)).astype(BF)
-    d_s4 = d_s4.astype(F32) + swap_core(d_s4).astype(F32)
-    last_sent = swap_core(last_send)
-    d_s4 = jnp.pad(jnp.where(own == 1, d_s4, 0.0), ((0, 0), (0, 128 - RS), (0, 0)))
-    last = last_mine.astype(F32) + last_sent.astype(F32) + d_s4
+    d_s4 = (d_s4.astype(F32) + after(d_s4_other, last_mine).astype(F32)).astype(BF)
+    d_s4 = jnp.where(own == 1, d_s4.astype(F32) + swap_core(d_s4).astype(F32), 0.0)
+    last = last_mine.astype(F32) + swap_core(last_send).astype(F32)
+    last = jnp.concatenate([last[:, :RS] + d_s4, last[:, RS:]], 1)
     if dp == SHARDS:
-        late_kept, late_out = halve(late_kept + after(late_in, last_sent))
+        late_kept, late_out = halve(late_kept + after(late_in, last_mine).astype(F32))
         last, late_out = lax.optimization_barrier((last, late_out))
-        late_in = send(late_out, 4)
-        for bit in (1, 2, 4):
+        late_in = send(late_out, LATE_SUM_BITS[2])
+        for bit in EARLY_SUM_BITS:
+            if bit == EARLY_SUM_BITS[1]:
+                last, late_in = lax.optimization_barrier((last, late_in))
             last_kept, last_out = halve(last)
-            last = last_kept + send(last_out, bit)
-        late_sum = (late_kept + after(late_in, last))[0]
+            last = last_kept + send(last_out, bit).astype(F32)
+        late_sum = (late_kept + late_in.astype(F32))[0]
         last = last[0]
     masters = (w_query, w_square, w_ffn_in, w_ffn_out, vectors)
     moments = (m_query, m_square, m_ffn_in, m_ffn_out, m_vectors)
@@ -1154,6 +1216,8 @@
         loss, outs = apply_updates(ids, (last, last_other, late_sum, late_other), masters, moments, averages)
     else:
         last, late = in_order(last, last_other, own), in_order(late_sum, late_other, own)
+        last = [jnp.stack([x[place(n, EARLY_SUM_BITS)] for n in range(SHARDS)]) for x in last]
+        late = [jnp.stack([x[place(n, LATE_SUM_BITS)] for n in range(SHARDS)]) for x in late]
         loss = lax.psum(late[0][0, 11 * RS : 11 * RS + 8, 0], "dp")
 
         def square(rows):

time: 195 us -> 189 us (0.969)
  other arithmetic: 12.2 us -> 8.46 us
  Pallas kernels: 104 us -> 107 us
  starting transfers between devices: 22.7 us -> 19.7 us
  local copies, waits for them, and re-layouts: 10.3 us -> 7.67 us
    pallas_call x0 -> x2, Pallas kernels: none -> 3.54 us  [the longest x1 1.88 us: pack_late(): pl.pallas_call(late_kernel, in_specs=[SM, VM, VM, VM], out_specs=VM, out_...]
    ppermute x6, starting transfers between devices: 6.31 us -> 3.94 us  [send(): return lax.ppermute(value, 'dp', pairs(SHARDS, bit))]
    ppermute x1, waiting for transfers between devices: 0.56 us -> 2.81 us  [gather_weights(): late = (late, lax.ppermute(late, 'dp', pairs(dp, LATE_BITS[1])))]
    unnamed x79 -> x88, local copies, waits for them, and re-layouts: 6.45 us -> 7.46 us
  transfers between devices with their start and end apart: 27 -> 27, of which waited for: 16 -> 15; matrix products, arithmetic and copies ran while one was open for 6% -> 4% of each run, Pallas kernels for 43% -> 46%
where the time goes in v2:
time: 189 us
  Pallas kernels  107 us (57%)
  waiting for transfers between devices  43.7 us (23%)
  starting transfers between devices  19.7 us (10%)
  other arithmetic  8.46 us (4%)
  local copies, waits for them, and re-layouts  7.67 us (4%)
    pallas_call x1, Pallas kernels, sample_backward(): pl.pallas_call(scatter_kernel, in_specs=[ANY, SM, SM, ANY] + [VM] * 4, ou...  33.2 us
    pallas_call x1, Pallas kernels, sample_forward(): pl.pallas_call(forward_kernel, in_specs=[ANY, SM, SM, ANY, VM, VM, VM], o...  30 us
    ppermute x6, waiting for transfers between devices, send(): return lax.ppermute(value, 'dp', pairs(SHARDS, bit))  20 us
    pallas_call x1, Pallas kernels, post_step(): pl.pallas_call(post_kernel, in_specs=[SM, SM, SM] + [VM] * 9, out_specs=[...  17.2 us
    pallas_call x1, Pallas kernels, front_backward(): pl.pallas_call(front_back_kernel, in_specs=[SM] + [VM] * 16, out_specs=[V...  9.8 us
    unnamed x88, local copies, waits for them, and re-layouts  7.46 us
    pallas_call x1, Pallas kernels, front_forward(): pl.pallas_call(front_kernel, in_specs=[SM, VM, VM, VM], out_specs=[VM] *...  7.15 us
    ppermute x12, waiting for transfers between devices, swap_core(): return lax.ppermute(value, 'level', pairs(4, 1))  5.65 us
  transfers between devices with their start and end apart: 27, of which 15 were waited for; matrix products, arithmetic and copies ran while one was open for 4% of the time, Pallas kernels for 46%

profile of v2, /device:TPU:0, one launch (start us, length us, event | category | flops | bytes accessed | tf_op | source)
XLA Modules:
  0.0 188.6 jit_solution(3304196423620780693)
XLA Ops:
  1.3 1.7 pack_early.1
  2.9 4.0 %collective-permute-start = (bf16[1,128,256]{2,1,0:T(8,128)(2,1)}, bf16[1,128,256]{2,1,0:T(8,128)(2,1)S(1)}, u32[]{:S(2)}, u32[]{:S(2)}) collective-permute-start(bf16[1,128,256]{2,1,0:T(8,128)(2,1)} %pack_early.1), channel_id=1, source_target_pairs={{0,16},{4,20},{8,24},{12,28},{16,0},{20,4},{24,8},{28,12},{1,17},{... | collective-permute-start | bytes 196616 | tf_op jit(solution)/shard_map/ppermute | solution.py:1095
  7.0 1.7 pick_rows.1.idx_ref
  8.7 1.9 pack_late.1
  11.7 1.4 collective-permute-start.1
  13.1 1.5 collective-permute-start.2
  14.6 2.1 %collective-permute-done.1 = bf16[2,128,256]{2,1,0:T(8,128)(2,1)S(1)} collective-permute-done((bf16[2,128,256]{2,1,0:T(8,128)(2,1)S(1)}, bf16[2,128,256]{2,1,0:T(8,128)(2,1)S(1)}, u32[]{:S(2)}, u32[]{:S(2)}) %collective-permute-start.1) | collective-permute-done | bytes 131104 | tf_op jit(solution)/shard_map/ppermute | solution.py:1098
  16.7 2.5 %collective-permute-done.2 = bf16[1,368,256]{2,1,0:T(8,128)(2,1)S(1)} collective-permute-done((bf16[1,368,256]{2,1,0:T(8,128)(2,1)}, bf16[1,368,256]{2,1,0:T(8,128)(2,1)S(1)}, u32[]{:S(2)}, u32[]{:S(2)}) %collective-permute-start.2) | collective-permute-done | bytes 188448 | tf_op jit(solution)/shard_map/ppermute | solution.py:1099
  19.2 1.5 collective-permute-start.3
  20.8 5.0 %collective-permute-done.3 = bf16[4,128,256]{2,1,0:T(8,128)(2,1)S(1)} collective-permute-done((bf16[4,128,256]{2,1,0:T(8,128)(2,1)S(1)}, bf16[4,128,256]{2,1,0:T(8,128)(2,1)S(1)}, u32[]{:S(2)}, u32[]{:S(2)}) %collective-permute-start.3) | collective-permute-done | bytes 262176 | tf_op jit(solution)/shard_map/ppermute | solution.py:1101
  27.9 7.2 %front_forward.1 = (bf16[4,256,256]{2,1,0:T(8,128)(2,1)}, bf16[256,384]{1,0:T(8,128)(2,1)}, bf16[256,256]{1,0:T(8,128)(2,1)}, f32[24,256]{1,0:T(8,128)}, f32[1,1...) custom-call(s32[4]{0:T(128)} %pad_add_fusion.ids_ref, ...), custom_call_target="tpu_custom_call" | custom-call | flops 1000000000 | bytes 5000000 | tf_op jit(solution)/shard_map/front_forward/pallas_call | solution.py:706
  35.2 2.8 %collective-permute-done.5 = bf16[2,368,256]{2,1,0:T(8,128)(2,1)S(1)} collective-permute-done((bf16[2,368,256]{2,1,0:T(8,128)(2,1)}, bf16[2,368,256]{2,1,0:T(8,128)(2,1)S(1)}, u32[]{:S(2)}, u32[]{:S(2)}) %collective-permute-start.5) | collective-permute-done | bytes 376864 | tf_op jit(solution)/shard_map/ppermute | solution.py:1103
  38.1 2.9 %collective-permute-start.9 = (bf16[4,368,256]{2,1,0:T(8,128)(2,1)S(1)}, bf16[4,368,256]{2,1,0:T(8,128)(2,1)S(1)}, u32[]{:S(2)}, u32[]{:S(2)}) collective-permute-start(bf16[4,368,256]{2,1,0:T(8,128)(2,1)S(1)} %constant_dynamic-update-slice_fusion.2.late_a), channel_id=1, source_target_pairs={{0,16},{4,20},{8,24},{12,28},{16,0},{20,4},{24,8},{28,12},{1,17},{... | collective-permute-start | bytes 2261000 | tf_op jit(solution)/shard_map/ppermute | solution.py:1163
  41.7 30.0 %sample_forward.1 = (bf16[8,1216,256]{2,1,0:T(8,128)(2,1)}, bf16[304,256]{1,0:T(8,128)(2,1)}, bf16[304,256]{1,0:T(8,128)(2,1)}) custom-call(s32[4,32,152]{2,1,0:T(8,128)} %pick_rows.1.idx_ref, s32[2,2]{1,0:T(2,128)} %size_ref.5, s32[4]{0:T(128)} %pad_add_fusion.ids_ref, bf16[1,16700,2,256]{3,2,1,0:T(2,128)(2,1)} %bitcast.18, ...), custom_call_target="tpu_custom_call" | custom-call | flops 30000001024 | bytes 60000000 | tf_op jit(solution)/shard_map/sample_forward/pallas_call | solution.py:330
  76.2 5.4 %collective-permute-done.8.add_ref = bf16[304,256]{1,0:T(8,128)(2,1)S(1)} collective-permute-done((bf16[304,256]{1,0:T(8,128)(2,1)S(1)}, bf16[304,256]{1,0:T(8,128)(2,1)S(1)}, u32[]{:S(2)}, u32[]{:S(2)}) %collective-permute-start.8) | collective-permute-done | bytes 155680 | tf_op jit(solution)/shard_map/ppermute | solution.py:1059
  82.8 1.1 copy-done.21
  84.9 17.2 %post_step.1 = (bf16[304,256]{1,0:T(8,128)(2,1)S(1)}, f32[304,256]{1,0:T(8,128)S(1)}, bf16[8,384,256]{2,1,0:T(8,128)(2,1)S(1)}, bf16[8,384,256]{2,1,0:T(8,128)(2,1)S(1)}, f32[24,256]{1,0:T(8,128)S(1)}) custom-call(s32[4]{0:T(128)S(1)} %copy-done.15, s32[2,32]{1,0:T(2,128)S(1)} %copy-done.26, s32[2]{0:T(128)S(1)} %copy-done.19, ...), custom_call_target="tpu_custom_call" | custom-call | flops 8000000000 | bytes 10000000 | tf_op jit(solution)/shard_map/post_step/pallas_call | solution.py:966
  102.2 1.4 collective-permute-done.12.ds_other
  103.8 2.4 %coef_backward.1 = (bf16[304,128]{1,0:T(8,128)(2,1)S(1)}, bf16[304,128]{1,0:T(8,128)(2,1)S(1)}) custom-call(s32[4]{0:T(128)S(1)} %copy-done.15, bf16[8,1216,256]{2,1,0:T(8,128)(2,1)S(1)} %copy-done.27, bf16[304,256]{1,0:T(8,128)(2,1)S(1)} %get-tuple-element.121.ds_mine, bf16[304,256]{1,0:T(8,128)(2,1)S(1)} %collective-permute-done.12.ds_other, ...), custom_call_target="tpu_custom_call" | custom-call | flops 2000000000 | bytes 10000000 | tf_op jit(solution)/shard_map/coef_backward/pallas_call | solution.py:396
  108.5 1.2 copy-done.36
  110.8 1.5 collective-permute-start.16
  112.3 33.2 %sample_backward.1 = bf16[8,32,256]{2,1,0:T(8,128)(2,1)} custom-call(s32[4,32,152]{2,1,0:T(8,128)} %pick_rows.1.idx_ref, s32[2,2]{1,0:T(2,128)} %size_ref.5, s32[4]{0:T(128)} %pad_add_fusion.ids_ref, bf16[1,16700,2,256]{3,2,1,0:T(2,128)(2,1)} %bitcast.19, bf16[304,256]{1,0:T(8,128)(2,1)} %copy-done.24, bf16[304,256]{1,0:T(8,128)(2,1)} %copy-done.25, ...), custom_call_target="tpu_custom_call" | custom-call | flops 30000001024 | bytes 60000000 | tf_op jit(solution)/shard_map/sample_backward/pallas_call | solution.py:495
  145.6 1.6 convert_add_fusion
  147.3 1.2 copy-done.33
  148.6 9.8 %front_backward.1 = (bf16[8,128,256]{2,1,0:T(8,128)(2,1)}, bf16[8,128,256]{2,1,0:T(8,128)(2,1)}) custom-call(s32[4]{0:T(128)} %pad_add_fusion.ids_ref, bf16[2,304,128]{2,1,0:T(8,128)(2,1)} %copy-done.38, bf16[2,304,128]{2,1,0:T(8,128)(2,1)} %copy-done.41, f32[304,128]{1,0:T(8,128)} %get-tuple-element.110.att_ref, f32[304,256]{1,0:T(8,128)} %copy-done.30, ...), custom_call_target="tpu_custom_call" | custom-call | flops 2000000000 | bytes 5000000 | tf_op jit(solution)/shard_map/front_backward/pallas_call | solution.py:770
  161.8 1.2 collective-permute-start.22
  163.0 7.1 %collective-permute-done.21 = bf16[4,128,256]{2,1,0:T(8,128)(2,1)S(1)} collective-permute-done((bf16[4,128,256]{2,1,0:T(8,128)(2,1)S(1)}, bf16[4,128,256]{2,1,0:T(8,128)(2,1)S(1)}, u32[]{:S(2)}, u32[]{:S(2)}) %collective-permute-start.21) | collective-permute-done | bytes 262176 | tf_op jit(solution)/shard_map/ppermute | solution.py:1137
  170.2 3.7 %collective-permute-done.22 = bf16[1,384,256]{2,1,0:T(8,128)(2,1)S(1)} collective-permute-done((bf16[1,384,256]{2,1,0:T(8,128)(2,1)S(1)}, bf16[1,384,256]{2,1,0:T(8,128)(2,1)S(1)}, u32[]{:S(2)}, u32[]{:S(2)}) %collective-permute-start.22) | collective-permute-done | bytes 196640 | tf_op jit(solution)/shard_map/ppermute | solution.py:1137
  174.0 5.0 %collective-permute-done.23 = bf16[2,128,256]{2,1,0:T(8,128)(2,1)S(1)} collective-permute-done((bf16[2,128,256]{2,1,0:T(8,128)(2,1)S(1)}, bf16[2,128,256]{2,1,0:T(8,128)(2,1)S(1)}, u32[]{:S(2)}, u32[]{:S(2)}) %collective-permute-start.23) | collective-permute-done | bytes 131104 | tf_op jit(solution)/shard_map/ppermute | solution.py:1137
  180.1 4.2 %collective-permute-done.24 = bf16[1,128,256]{2,1,0:T(8,128)(2,1)S(1)} collective-permute-done((bf16[1,128,256]{2,1,0:T(8,128)(2,1)S(1)}, bf16[1,128,256]{2,1,0:T(8,128)(2,1)S(1)}, u32[]{:S(2)}, u32[]{:S(2)}) %collective-permute-start.24) | collective-permute-done | bytes 65568 | tf_op jit(solution)/shard_map/ppermute | solution.py:1137
  184.5 1.3 collective-permute-done.25.last_other
  185.9 2.4 %apply_updates.1 = (f32[1,1]{1,0:T(1,128)}, f32[32,384]{1,0:T(8,128)}, bf16[32,384]{1,0:T(8,128)(2,1)}, f32[32,384]{1,0:T(8,128)}, f32[32,384]{1,0:T(8,128)}, /*...) custom-call(s32[4]{0:T(128)S(1)} %copy-done.16, ...), custom_call_target="tpu_custom_call" | custom-call | flops 3000000 | bytes 8000000 | tf_op jit(solution)/shard_map/apply_updates/pallas_call | solution.py:1038
  (145 shorter events, 19.8 us)
Async XLA Ops:
  2.9 7.9 %collective-permute-start = (bf16[1,128,256]{2,1,0:T(8,128)(2,1)}, bf16[1,128,256]{2,1,0:T(8,128)(2,1)S(1)}, u32[]{:S(2)}, u32[]{:S(2)}) collective-permute-start(bf16[1,128,256]{2,1,0:T(8,128)(2,1)} %pack_early.1), channel_id=1, source_target_pairs={{0,16},{4,20},{8,24},{12,28},{16,0},{20,4},{24,8},{28,12},{1,17},{... | collective-permute-start | bytes 196616 | tf_op jit(solution)/shard_map/ppermute | solution.py:1095
  11.7 5.0 %collective-permute-start.1 = (bf16[2,128,256]{2,1,0:T(8,128)(2,1)S(1)}, bf16[2,128,256]{2,1,0:T(8,128)(2,1)S(1)}, u32[]{:S(2)}, u32[]{:S(2)}) collective-permute-start(bf16[2,128,256]{2,1,0:T(8,128)(2,1)S(1)} %pad_maximum_fusion.4), channel_id=1, source_target_pairs={{0,8},{4,12},{8,0},{12,4},{16,24},{20,28},{24,16},{28,20},{1,9},{5... | collective-permute-start | bytes 393224 | tf_op jit(solution)/shard_map/ppermute | solution.py:1098
  13.1 6.1 %collective-permute-start.2 = (bf16[1,368,256]{2,1,0:T(8,128)(2,1)}, bf16[1,368,256]{2,1,0:T(8,128)(2,1)S(1)}, u32[]{:S(2)}, u32[]{:S(2)}) collective-permute-start(bf16[1,368,256]{2,1,0:T(8,128)(2,1)} %pack_late.1), channel_id=1, source_target_pairs={{0,4},{4,0},{8,12},{12,8},{16,20},{20,16},{24,28},{28,24},{1,5},{5... | collective-permute-start | bytes 565256 | tf_op jit(solution)/shard_map/ppermute | solution.py:1099
  19.2 6.6 %collective-permute-start.3 = (bf16[4,128,256]{2,1,0:T(8,128)(2,1)S(1)}, bf16[4,128,256]{2,1,0:T(8,128)(2,1)S(1)}, u32[]{:S(2)}, u32[]{:S(2)}) collective-permute-start(bf16[4,128,256]{2,1,0:T(8,128)(2,1)S(1)} %pad_maximum_fusion.2), channel_id=1, source_target_pairs={{0,4},{4,0},{8,12},{12,8},{16,20},{20,16},{24,28},{28,24},{1,5},{5... | collective-permute-start | bytes 786440 | tf_op jit(solution)/shard_map/ppermute | solution.py:1101
  25.8 2.1 %collective-permute-start.4 = (bf16[8,128,256]{2,1,0:T(8,128)(2,1)S(1)}, bf16[8,128,256]{2,1,0:T(8,128)(2,1)}, u32[]{:S(2)}, u32[]{:S(2)}) collective-permute-start(bf16[8,128,256]{2,1,0:T(8,128)(2,1)S(1)} %constant_dynamic-update-slice_fusion.mine_ref), channel_id=1, source_target_pairs={{0,1},{1,0},{2,3},{3,2},{4,5},{5,4},{6,7},{7,6},{8,9},{9,8},{10,11... | collective-permute-start | bytes 1572872 | tf_op jit(solution)/shard_map/ppermute | solution.py:1055
  26.7 11.3 %collective-permute-start.5 = (bf16[2,368,256]{2,1,0:T(8,128)(2,1)}, bf16[2,368,256]{2,1,0:T(8,128)(2,1)S(1)}, u32[]{:S(2)}, u32[]{:S(2)}) collective-permute-start(bf16[2,368,256]{2,1,0:T(8,128)(2,1)} %pad_maximum_fusion.1), channel_id=1, source_target_pairs={{0,8},{4,12},{8,0},{12,4},{16,24},{20,28},{24,16},{28,20},{1,9},{5... | collective-permute-start | bytes 1130504 | tf_op jit(solution)/shard_map/ppermute | solution.py:1103
  35.1 5.9 %collective-permute-start.6 = (f32[304,128]{1,0:T(8,128)}, f32[304,128]{1,0:T(8,128)S(1)}, u32[]{:S(2)}, u32[]{:S(2)}) collective-permute-start(f32[304,128]{1,0:T(8,128)} %get-tuple-element.114), channel_id=1, source_target_pairs={{0,1},{1,0},{2,3},{3,2},{4,5},{5,4},{6,7},{7,6},{8,9},{9,8},{10,11... | collective-permute-start | bytes 466952 | tf_op jit(solution)/shard_map/ppermute | solution.py:1055
  38.1 36.2 %collective-permute-start.9 = (bf16[4,368,256]{2,1,0:T(8,128)(2,1)S(1)}, bf16[4,368,256]{2,1,0:T(8,128)(2,1)S(1)}, u32[]{:S(2)}, u32[]{:S(2)}) collective-permute-start(bf16[4,368,256]{2,1,0:T(8,128)(2,1)S(1)} %constant_dynamic-update-slice_fusion.2.late_a), channel_id=1, source_target_pairs={{0,16},{4,20},{8,24},{12,28},{16,0},{20,4},{24,8},{28,12},{1,17},{... | collective-permute-start | bytes 2261000 | tf_op jit(solution)/shard_map/ppermute | solution.py:1163
  41.6 40.0 %copy-start.15 = (s32[4]{0:T(128)S(1)}, s32[4]{0:T(128)}, u32[]{:S(2)}) copy-start(s32[4]{0:T(128)} %pad_add_fusion.ids_ref) | copy-start | bytes 52
  41.6 40.1 %copy-start.19 = (s32[2]{0:T(128)S(1)}, s32[2]{0:T(128)}, u32[]{:S(2)}) copy-start(s32[2]{0:T(128)} %count_ref.3) | copy-start | bytes 28
  41.6 40.1 %copy-start.26 = (s32[2,32]{1,0:T(2,128)S(1)}, s32[2,32]{1,0:T(2,128)}, u32[]{:S(2)}) copy-start(s32[2,32]{1,0:T(2,128)} %match_ref.1) | copy-start | bytes 772
  41.7 40.1 %copy-start.31 = (f32[24,256]{1,0:T(8,128)S(1)}, f32[24,256]{1,0:T(8,128)}, u32[]{:S(2)}) copy-start(f32[24,256]{1,0:T(8,128)} %get-tuple-element.120.vec_ref) | copy-start | bytes 73732
  71.7 1.7 collective-permute-start.7
  71.8 9.9 %collective-permute-start.10 = (bf16[4,368,256]{2,1,0:T(8,128)(2,1)S(1)}, bf16[4,368,256]{2,1,0:T(8,128)(2,1)S(1)}, u32[]{:S(2)}, u32[]{:S(2)}) collective-permute-start(bf16[4,368,256]{2,1,0:T(8,128)(2,1)S(1)} %constant_dynamic-update-slice_fusion.2.late_a), channel_id=1, source_target_pairs={{0,1},{1,0},{2,3},{3,2},{4,5},{5,4},{6,7},{7,6},{8,9},{9,8},{10,11... | collective-permute-start | bytes 2261000 | tf_op jit(solution)/shard_map/ppermute | solution.py:1055
  74.3 7.4 %collective-permute-start.11 = (bf16[4,368,256]{2,1,0:T(8,128)(2,1)S(1)}, bf16[4,368,256]{2,1,0:T(8,128)(2,1)}, u32[]{:S(2)}, u32[]{:S(2)}) collective-permute-start(bf16[4,368,256]{2,1,0:T(8,128)(2,1)S(1)} %collective-permute-done.9.late_b), channel_id=1, source_target_pairs={{0,1},{1,0},{2,3},{3,2},{4,5},{5,4},{6,7},{7,6},{8,9},{9,8},{10,11... | collective-permute-start | bytes 2261000 | tf_op jit(solution)/shard_map/ppermute | solution.py:1055
  75.4 6.3 %collective-permute-start.8 = (bf16[304,256]{1,0:T(8,128)(2,1)S(1)}, bf16[304,256]{1,0:T(8,128)(2,1)S(1)}, u32[]{:S(2)}, u32[]{:S(2)}) collective-permute-start(bf16[304,256]{1,0:T(8,128)(2,1)S(1)} %add_convert_fusion.1.s_ref), channel_id=1, source_target_pairs={{0,2},{1,3},{2,0},{3,1},{4,6},{5,7},{6,4},{7,5},{8,10},{9,11},{10,... | collective-permute-start | bytes 466952 | tf_op jit(solution)/shard_map/ppermute | solution.py:1059
  102.2 1.4 collective-permute-start.12
  103.6 4.9 %collective-permute-start.14 = (bf16[8,384,256]{2,1,0:T(8,128)(2,1)S(1)}, bf16[8,384,256]{2,1,0:T(8,128)(2,1)S(1)}, u32[]{:S(2)}, u32[]{:S(2)}) collective-permute-start(bf16[8,384,256]{2,1,0:T(8,128)(2,1)S(1)} %get-tuple-element.126), channel_id=1, source_target_pairs={{0,1},{1,0},{2,3},{3,2},{4,5},{5,4},{6,7},{7,6},{8,9},{9,8},{10,11... | collective-permute-start | bytes 4718600 | tf_op jit(solution)/shard_map/ppermute | solution.py:1055
  106.2 1.4 collective-permute-start.13
  107.5 38.0 %copy-start.38 = (bf16[2,304,128]{2,1,0:T(8,128)(2,1)}, bf16[2,304,128]{2,1,0:T(8,128)(2,1)S(1)}, u32[]{:S(2)}) copy-start(bf16[2,304,128]{2,1,0:T(8,128)(2,1)S(1)} %pad_maximum_fusion.3.near_ref) | copy-start | bytes 466948
  107.6 38.0 %collective-permute-start.15 = (bf16[2,304,128]{2,1,0:T(8,128)(2,1)S(1)}, bf16[2,304,128]{2,1,0:T(8,128)(2,1)S(1)}, u32[]{:S(2)}, u32[]{:S(2)}) collective-permute-start(bf16[2,304,128]{2,1,0:T(8,128)(2,1)S(1)} %pad_maximum_fusion.3.near_ref), channel_id=1, source_target_pairs={{0,2},{1,3},{2,0},{3,1},{4,6},{5,7},{6,4},{7,5},{8,10},{9,11},{10,... | collective-permute-start | bytes 466952 | tf_op jit(solution)/shard_map/ppermute | solution.py:1059
  110.8 34.7 %collective-permute-start.16 = (bf16[4,384,256]{2,1,0:T(8,128)(2,1)}, bf16[4,384,256]{2,1,0:T(8,128)(2,1)}, u32[]{:S(2)}, u32[]{:S(2)}) collective-permute-start(bf16[4,384,256]{2,1,0:T(8,128)(2,1)} %add_convert_fusion), channel_id=1, source_target_pairs={{0,4},{4,0},{8,12},{12,8},{16,20},{20,16},{24,28},{28,24},{1,5},{5... | collective-permute-start | bytes 2359304 | tf_op jit(solution)/shard_map/ppermute | solution.py:1137
  145.5 12.9 %collective-permute-start.18 = (bf16[8,32,256]{2,1,0:T(8,128)(2,1)}, bf16[8,32,256]{2,1,0:T(8,128)(2,1)}, u32[]{:S(2)}, u32[]{:S(2)}) collective-permute-start(bf16[8,32,256]{2,1,0:T(8,128)(2,1)} %sample_backward.1), channel_id=1, source_target_pairs={{0,2},{1,3},{2,0},{3,1},{4,6},{5,7},{6,4},{7,5},{8,10},{9,11},{10,... | collective-permute-start | bytes 393224 | tf_op jit(solution)/shard_map/ppermute | solution.py:1059
  148.5 11.5 %collective-permute-start.20 = (bf16[2,384,256]{2,1,0:T(8,128)(2,1)S(1)}, bf16[2,384,256]{2,1,0:T(8,128)(2,1)}, u32[]{:S(2)}, u32[]{:S(2)}) collective-permute-start(bf16[2,384,256]{2,1,0:T(8,128)(2,1)S(1)} %slice.100), channel_id=1, source_target_pairs={{0,8},{4,12},{8,0},{12,4},{16,24},{20,28},{24,16},{28,20},{1,9},{5... | collective-permute-start | bytes 1179656 | tf_op jit(solution)/shard_map/ppermute | solution.py:1137
  158.4 2.8 %collective-permute-start.17 = (bf16[8,128,256]{2,1,0:T(8,128)(2,1)}, bf16[8,128,256]{2,1,0:T(8,128)(2,1)S(1)}, u32[]{:S(2)}, u32[]{:S(2)}) collective-permute-start(bf16[8,128,256]{2,1,0:T(8,128)(2,1)} %get-tuple-element.145), channel_id=1, source_target_pairs={{0,1},{1,0},{2,3},{3,2},{4,5},{5,4},{6,7},{7,6},{8,9},{9,8},{10,11... | collective-permute-start | bytes 1572872 | tf_op jit(solution)/shard_map/ppermute | solution.py:1055
  159.5 1.8 collective-permute-start.19
  161.7 8.4 %collective-permute-start.21 = (bf16[4,128,256]{2,1,0:T(8,128)(2,1)S(1)}, bf16[4,128,256]{2,1,0:T(8,128)(2,1)S(1)}, u32[]{:S(2)}, u32[]{:S(2)}) collective-permute-start(bf16[4,128,256]{2,1,0:T(8,128)(2,1)S(1)} %slice.101), channel_id=1, source_target_pairs={{0,4},{4,0},{8,12},{12,8},{16,20},{20,16},{24,28},{28,24},{1,5},{5... | collective-permute-start | bytes 786440 | tf_op jit(solution)/shard_map/ppermute | solution.py:1137
  161.8 12.1 %collective-permute-start.22 = (bf16[1,384,256]{2,1,0:T(8,128)(2,1)S(1)}, bf16[1,384,256]{2,1,0:T(8,128)(2,1)S(1)}, u32[]{:S(2)}, u32[]{:S(2)}) collective-permute-start(bf16[1,384,256]{2,1,0:T(8,128)(2,1)S(1)} %slice.102), channel_id=1, source_target_pairs={{0,16},{4,20},{8,24},{12,28},{16,0},{20,4},{24,8},{28,12},{1,17},{... | collective-permute-start | bytes 589832 | tf_op jit(solution)/shard_map/ppermute | solution.py:1137
  173.9 5.0 %collective-permute-start.23 = (bf16[2,128,256]{2,1,0:T(8,128)(2,1)S(1)}, bf16[2,128,256]{2,1,0:T(8,128)(2,1)S(1)}, u32[]{:S(2)}, u32[]{:S(2)}) collective-permute-start(bf16[2,128,256]{2,1,0:T(8,128)(2,1)S(1)} %slice.103), channel_id=1, source_target_pairs={{0,8},{4,12},{8,0},{12,4},{16,24},{20,28},{24,16},{28,20},{1,9},{5... | collective-permute-start | bytes 393224 | tf_op jit(solution)/shard_map/ppermute | solution.py:1137
  179.0 5.4 %collective-permute-start.24 = (bf16[1,128,256]{2,1,0:T(8,128)(2,1)S(1)}, bf16[1,128,256]{2,1,0:T(8,128)(2,1)S(1)}, u32[]{:S(2)}, u32[]{:S(2)}) collective-permute-start(bf16[1,128,256]{2,1,0:T(8,128)(2,1)S(1)} %slice.104), channel_id=1, source_target_pairs={{0,16},{4,20},{8,24},{12,28},{16,0},{20,4},{24,8},{28,12},{1,17},{... | collective-permute-start | bytes 196616 | tf_op jit(solution)/shard_map/ppermute | solution.py:1137
  180.0 5.7 %collective-permute-start.26 = (f32[384,256]{1,0:T(8,128)S(1)}, f32[384,256]{1,0:T(8,128)S(1)}, u32[]{:S(2)}, u32[]{:S(2)}) collective-permute-start(f32[384,256]{1,0:T(8,128)S(1)} %fusion.late_mine), channel_id=1, source_target_pairs={{0,1},{1,0},{2,3},{3,2},{4,5},{5,4},{6,7},{7,6},{8,9},{9,8},{10,11... | collective-permute-start | bytes 1179656 | tf_op jit(solution)/shard_map/ppermute | solution.py:1055
  184.4 1.4 collective-permute-start.25
  (37 other events, 567.2 us)
